TPU v7x, 32 devices: a whole 2x2x4 slice. The times are simulated.
32 devices in a mesh: row: 2 (over y), col: 8 (over z, x), layer: 2 (over core).
Axes of the slice: x: 2, y: 2, z: 4, core: 2. Of those that a mesh axis runs over, the one named last changes fastest.
Arguments:
- s_values: bfloat16 [2, 8, 2, 128, 128], P('row', 'col'), may hold values from -0.5 to 0.5
- s_slots: int32 [2, 8, 2], P('row', 'col'), may hold values from 0 to 16, as said below
- x_values: bfloat16 [4, 2, 8, 1, 128, 128], P(None, 'row', 'col'), may hold values from -6 to 6
- x_slots: int32 [4, 2, 8, 1], P(None, 'row', 'col'), may hold values from 0 to 3, as said below
Outputs:
- product: float32 [2048, 2048], P(('row', 'layer'), 'col')
Inputs may be any that keep to these rules, and one draw needn't show every extreme that they name: `s_slots`: within one piece the live values are distinct; the value 8 * 2 marks an empty slot, empty slots follow the live ones, every piece has at least one live slot, and at least one piece has all 2 slots live. `x_slots`: within one piece the 1 positions are distinct.
All inputs are finite; a program needn't handle non-finite values.
Results may differ from a plain program's by a relative error of at most 0.0003.
Values may be sent and summed in bfloat16 or wider, within the bound.
No kernel may reach another device: no remote copies, remote signals or barrier semaphores. Data moves between devices by JAX's collectives and lax.ppermute only.
A program may use at most 64 MiB of HBM per device.

v0:
```python
import jax
import jax.numpy as jnp
from jax import lax
from jax.sharding import PartitionSpec as P

BR = 8
BC = 2


def for_sending(value):

    def short(part):
        return part.astype(jnp.bfloat16) if part.dtype == jnp.float32 else part

    return jax.tree.map(short, value)


def passed_along(value, axis, by):
    count = lax.axis_size(axis)
    return lax.ppermute(value, axis, [(i, (i + by) % count) for i in range(count)])


def bit_count(value):
    return value.bit_length()


def align(held, amount, width, levels, axis_kind):
    for level in range(levels):
        distance = (1 << level) % width
        if axis_kind == "col_full":
            moved = jax.tree.map(
                lambda part, own: part.astype(own.dtype),
                passed_along(for_sending(held), "col", width - distance),
                held,
            )
        else:
            moved = jax.tree.map(
                lambda part, own: part.astype(own.dtype),
                passed_along(for_sending(held), "row", width - distance),
                held,
            )
        taken = amount >> level & 1 == 1
        held = jax.tree.map(lambda fresh, stale: jnp.where(taken, fresh, stale), moved, held)
    return held


def expand_density(piece_values, piece_slots, inner, block):
    kx_count = piece_slots.shape[0]
    columns = BC
    one_hot = (
        piece_slots[None, :] == jnp.arange(inner * columns, dtype=jnp.int32)[:, None]
    ).astype(jnp.bfloat16)
    flat = jnp.dot(
        one_hot, piece_values.reshape(kx_count, block * block), preferred_element_type=jnp.float32
    )
    tiles = flat.astype(jnp.bfloat16).reshape(inner, columns, block, block)
    return tiles.transpose(0, 2, 1, 3).reshape(inner * block, columns * block)


def dense_kernel(total, s_piece, s_pos, x_tile, inner, block):
    ks_count = s_pos.shape[0]
    one_hot = (s_pos[None, :] == jnp.arange(BR * inner, dtype=jnp.int32)[:, None]).astype(
        jnp.bfloat16
    )
    flat = jnp.dot(
        one_hot, s_piece.reshape(ks_count, block * block), preferred_element_type=jnp.float32
    )
    tiles = flat.astype(jnp.bfloat16).reshape(BR, inner, block, block)
    s_tile = tiles.transpose(0, 2, 1, 3).reshape(BR * block, inner * block)
    return total + jnp.dot(s_tile, x_tile, preferred_element_type=jnp.float32)


def per_device(s_values, s_slots, x_values, x_slots):
    n_row = lax.axis_size("row")
    n_col = lax.axis_size("col")
    n_layer = lax.axis_size("layer")
    row_id = lax.axis_index("row")
    col_id = lax.axis_index("col")
    layer_id = lax.axis_index("layer")
    per_layer = n_col // n_layer
    inner = n_row * BR // n_col
    block = s_values.shape[-1]
    held_s = (s_values[0, 0], s_slots[0, 0])
    s_offset = row_id + layer_id * per_layer
    held_s = align(held_s, s_offset % n_col, n_col, bit_count(n_col - 1), "col_full")
    shift_x = (col_id + layer_id * per_layer) % n_row
    held_x = align(
        (x_values[:, 0, 0], x_slots[:, 0, 0]), shift_x, n_row, bit_count(n_row - 1), "row_full"
    )
    start_piece = col_id + row_id + layer_id * per_layer
    total = jnp.zeros((BR * block, BC * block), jnp.float32)
    for turn in range(per_layer):
        piece = (start_piece + turn) % n_col
        group_pick = piece // n_row
        piece_values = lax.dynamic_index_in_dim(held_x[0], group_pick, 0, keepdims=False)
        piece_slots = lax.dynamic_index_in_dim(held_x[1], group_pick, 0, keepdims=False)
        x_tile = expand_density(piece_values, piece_slots, inner, block)
        total = dense_kernel(total, held_s[0], held_s[1], x_tile, inner, block)
        if turn + 1 < per_layer:
            held_s = jax.tree.map(
                lambda part, own: part.astype(own.dtype),
                passed_along(for_sending(held_s), "col", n_col - 1),
                held_s,
            )
            held_x = jax.tree.map(
                lambda part, own: part.astype(own.dtype),
                passed_along(for_sending(held_x), "row", n_row - 1),
                held_x,
            )
    return lax.psum_scatter(total, "layer", scatter_dimension=0, tiled=True)


def solution(mesh):
    placed = (
        P("row", "col", None, None, None),
        P("row", "col", None),
        P(None, "row", "col", None, None, None),
        P(None, "row", "col", None),
    )
    return jax.shard_map(
        per_device,
        mesh=mesh,
        in_specs=placed,
        out_specs=P(("row", "layer"), "col"),
        check_vma=False,
    )
```

profile of v0, /device:TPU:0, one launch (start us, length us, event | category | flops | bytes accessed | tf_op | source)
XLA Modules:
  0.0 96.9 jit_solution(17664566394875117146)
XLA Ops:
  6.5 6.0 %collective-permute-start.3 = (bf16[2,128,128]{2,1,0:T(8,128)(2,1)}, bf16[2,128,128]{2,1,0:T(8,128)(2,1)S(1)}, u32[]{:S(2)}, u32[]{:S(2)}) collective-permute-start(bf16[2,128,128]{2,1,0:T(8,128)(2,1)} %bitcast.158), channel_id=1, source_target_pairs={{0,14},{2,0},{4,2},{6,4},{8,6},{10,8},{12,10},{14,12},{1,15},{3,1}... | collective-permute-start | bytes 196616 | tf_op jit(solution)/shard_map/ppermute | solution.py:20
  12.5 0.7 collective-permute-start
  13.2 1.5 %collective-permute-start.7 = (bf16[4,1,128,128]{3,2,0,1:T(8,128)(2,1)}, bf16[4,1,128,128]{3,2,0,1:T(8,128)(2,1)S(1)}, u32[]{:S(2)}, u32[]{:S(2)}) collective-permute-start(bf16[4,1,128,128]{3,2,0,1:T(8,128)(2,1)} %bitcast.157), channel_id=1, source_target_pairs={{0,16},{16,0},{1,17},{17,1},{2,18},{18,2},{3,19},{19,3},{4,20},{20... | collective-permute-start | bytes 393224 | tf_op jit(solution)/shard_map/ppermute | solution.py:20
  14.7 0.7 collective-permute-start.6
  15.3 0.7 collective-permute-done
  16.1 0.4 collective-permute-start.1
  16.5 3.1 %collective-permute-done.1 = s32[2]{0:T(128)S(1)} collective-permute-done((s32[2]{0:T(128)S(1)}, s32[2]{0:T(128)S(1)}, u32[]{:S(2)}, u32[]{:S(2)}) %collective-permute-start.1) | collective-permute-done | bytes 40 | tf_op jit(solution)/shard_map/ppermute | solution.py:20
  19.6 0.0 collective-permute-start.2
  19.6 1.6 %collective-permute-start.10 = (s32[4,1]{0,1:T(1,128)S(1)}, s32[4,1]{0,1:T(1,128)S(1)}, u32[]{:S(2)}, u32[]{:S(2)}) collective-permute-start(s32[4,1]{0,1:T(1,128)S(1)} %broadcast_select_fusion.4), channel_id=1, source_target_pairs={{0,16},{16,0},{1,17},{17,1},{2,18},{18,2},{3,19},{19,3},{4,20},{20... | collective-permute-start | bytes 56 | tf_op jit(solution)/shard_map/ppermute | solution.py:20
  21.2 0.6 constant_dynamic-slice_fusion.3
  21.8 0.6 fusion.37
  22.5 1.6 %collective-permute-done.2 = s32[2]{0:T(128)S(1)} collective-permute-done((s32[2]{0:T(128)S(1)}, s32[2]{0:T(128)S(1)}, u32[]{:S(2)}, u32[]{:S(2)}) %collective-permute-start.2) | collective-permute-done | bytes 40 | tf_op jit(solution)/shard_map/ppermute | solution.py:20
  24.1 5.5 %collective-permute-start.8 = (s32[2]{0:T(128)S(1)}, s32[2]{0:T(128)S(1)}, u32[]{:S(2)}, u32[]{:S(2)}) collective-permute-start(s32[2]{0:T(128)S(1)} %broadcast_select_fusion.7), channel_id=1, source_target_pairs={{0,14},{2,0},{4,2},{6,4},{8,6},{10,8},{12,10},{14,12},{1,15},{3,1}... | collective-permute-start | bytes 32 | tf_op jit(solution)/shard_map/ppermute | solution.py:20
  29.5 0.6 constant_dynamic-slice_fusion.2
  30.1 0.6 fusion.38
  30.8 1.6 %collective-permute-start.14 = (s32[4,1]{0,1:T(1,128)S(1)}, s32[4,1]{0,1:T(1,128)S(1)}, u32[]{:S(2)}, u32[]{:S(2)}) collective-permute-start(s32[4,1]{0,1:T(1,128)S(1)} %collective-permute-done.10), channel_id=1, source_target_pairs={{0,16},{16,0},{1,17},{17,1},{2,18},{18,2},{3,19},{19,3},{4,20},{20... | collective-permute-start | bytes 56 | tf_op jit(solution)/shard_map/ppermute | solution.py:20
  32.4 3.4 %collective-permute-start.12 = (s32[2]{0:T(128)S(1)}, s32[2]{0:T(128)S(1)}, u32[]{:S(2)}, u32[]{:S(2)}) collective-permute-start(s32[2]{0:T(128)S(1)} %collective-permute-done.8), channel_id=1, source_target_pairs={{0,14},{2,0},{4,2},{6,4},{8,6},{10,8},{12,10},{14,12},{1,15},{3,1}... | collective-permute-start | bytes 32 | tf_op jit(solution)/shard_map/ppermute | solution.py:20
  35.8 1.3 %collective-permute-done.12 = s32[2]{0:T(128)S(1)} collective-permute-done((s32[2]{0:T(128)S(1)}, s32[2]{0:T(128)S(1)}, u32[]{:S(2)}, u32[]{:S(2)}) %collective-permute-start.12) | collective-permute-done | bytes 40 | tf_op jit(solution)/shard_map/ppermute | solution.py:20
  37.1 4.9 %collective-permute-start.16 = (s32[2]{0:T(128)S(1)}, s32[2]{0:T(128)S(1)}, u32[]{:S(2)}, u32[]{:S(2)}) collective-permute-start(s32[2]{0:T(128)S(1)} %collective-permute-done.12), channel_id=1, source_target_pairs={{0,14},{2,0},{4,2},{6,4},{8,6},{10,8},{12,10},{14,12},{1,15},{3,1}... | collective-permute-start | bytes 32 | tf_op jit(solution)/shard_map/ppermute | solution.py:20
  42.0 0.6 constant_dynamic-slice_fusion.1
  42.6 0.6 fusion.39
  43.3 1.6 %collective-permute-start.18 = (s32[4,1]{0,1:T(1,128)S(1)}, s32[4,1]{0,1:T(1,128)S(1)}, u32[]{:S(2)}, u32[]{:S(2)}) collective-permute-start(s32[4,1]{0,1:T(1,128)S(1)} %collective-permute-done.14), channel_id=1, source_target_pairs={{0,16},{16,0},{1,17},{17,1},{2,18},{18,2},{3,19},{19,3},{4,20},{20... | collective-permute-start | bytes 56 | tf_op jit(solution)/shard_map/ppermute | solution.py:20
  44.8 2.0 %collective-permute-done.18 = s32[4,1]{0,1:T(1,128)S(1)} collective-permute-done((s32[4,1]{0,1:T(1,128)S(1)}, s32[4,1]{0,1:T(1,128)S(1)}, u32[]{:S(2)}, u32[]{:S(2)}) %collective-permute-start.18) | collective-permute-done | bytes 48 | tf_op jit(solution)/shard_map/ppermute | solution.py:20
  46.9 0.6 constant_dynamic-slice_fusion
  47.4 0.6 fusion.40
  48.1 0.1 collective-permute-start.4
  48.3 1.6 %collective-permute-start.11 = (bf16[4,1,128,128]{3,2,0,1:T(8,128)(2,1)S(1)}, bf16[4,1,128,128]{3,2,0,1:T(8,128)(2,1)S(1)}, u32[]{:S(2)}, u32[]{:S(2)}) collective-permute-start(bf16[4,1,128,128]{3,2,0,1:T(8,128)(2,1)S(1)} %broadcast_select_fusion), channel_id=1, source_target_pairs={{0,16},{16,0},{1,17},{17,1},{2,18},{18,2},{3,19},{19,3},{4,20},{20... | collective-permute-start | bytes 393224 | tf_op jit(solution)/shard_map/ppermute | solution.py:20
  49.9 2.6 %collective-permute-done.4 = bf16[2,128,128]{2,1,0:T(8,128)(2,1)S(1)} collective-permute-done((bf16[2,128,128]{2,1,0:T(8,128)(2,1)S(1)}, bf16[2,128,128]{2,1,0:T(8,128)(2,1)S(1)}, u32[]{:S(2)}, u32[]{:S(2)}) %collective-permute-start.4) | collective-permute-done | bytes 65568 | tf_op jit(solution)/shard_map/ppermute | solution.py:20
  52.5 0.1 collective-permute-start.5
  52.6 0.1 fusion.13
  52.7 0.1 copy.10
  52.8 5.1 %collective-permute-done.5 = bf16[2,128,128]{2,1,0:T(8,128)(2,1)S(1)} collective-permute-done((bf16[2,128,128]{2,1,0:T(8,128)(2,1)S(1)}, bf16[2,128,128]{2,1,0:T(8,128)(2,1)S(1)}, u32[]{:S(2)}, u32[]{:S(2)}) %collective-permute-start.5) | collective-permute-done | bytes 65568 | tf_op jit(solution)/shard_map/ppermute | solution.py:20
  57.9 1.6 %collective-permute-start.9 = (bf16[2,128,128]{2,1,0:T(8,128)(2,1)S(1)}, bf16[2,128,128]{2,1,0:T(8,128)(2,1)S(1)}, u32[]{:S(2)}, u32[]{:S(2)}) collective-permute-start(bf16[2,128,128]{2,1,0:T(8,128)(2,1)S(1)} %broadcast_select_fusion.3), channel_id=1, source_target_pairs={{0,14},{2,0},{4,2},{6,4},{8,6},{10,8},{12,10},{14,12},{1,15},{3,1}... | collective-permute-start | bytes 196616 | tf_op jit(solution)/shard_map/ppermute | solution.py:20
  59.6 0.3 fusion
  59.9 0.1 copy.18
  60.0 0.3 copy.9
  60.3 0.3 fusion.10
  60.6 2.1 %collective-permute-done.9 = bf16[2,128,128]{2,1,0:T(8,128)(2,1)S(1)} collective-permute-done((bf16[2,128,128]{2,1,0:T(8,128)(2,1)S(1)}, bf16[2,128,128]{2,1,0:T(8,128)(2,1)S(1)}, u32[]{:S(2)}, u32[]{:S(2)}) %collective-permute-start.9) | collective-permute-done | bytes 65568 | tf_op jit(solution)/shard_map/ppermute | solution.py:20
  62.8 0.3 fusion.1
  63.0 0.1 copy.23
  63.1 0.3 copy.11
  63.5 0.1 fusion.14
  63.6 0.1 copy.12
  63.8 3.8 %collective-permute-start.13 = (bf16[2,128,128]{2,1,0:T(8,128)(2,1)S(1)}, bf16[2,128,128]{2,1,0:T(8,128)(2,1)S(1)}, u32[]{:S(2)}, u32[]{:S(2)}) collective-permute-start(bf16[2,128,128]{2,1,0:T(8,128)(2,1)S(1)} %collective-permute-done.9), channel_id=1, source_target_pairs={{0,14},{2,0},{4,2},{6,4},{8,6},{10,8},{12,10},{14,12},{1,15},{3,1}... | collective-permute-start | bytes 196616 | tf_op jit(solution)/shard_map/ppermute | solution.py:20
  67.6 1.5 %collective-permute-start.15 = (bf16[4,1,128,128]{3,2,0,1:T(8,128)(2,1)S(1)}, bf16[4,1,128,128]{3,2,0,1:T(8,128)(2,1)S(1)}, u32[]{:S(2)}, u32[]{:S(2)}) collective-permute-start(bf16[4,1,128,128]{3,2,0,1:T(8,128)(2,1)S(1)} %collective-permute-done.11), channel_id=1, source_target_pairs={{0,16},{16,0},{1,17},{17,1},{2,18},{18,2},{3,19},{19,3},{4,20},{20... | collective-permute-start | bytes 393224 | tf_op jit(solution)/shard_map/ppermute | solution.py:20
  69.1 0.4 convolution_add_fusion.2
  69.5 0.0 collective-permute-done.13
  69.5 0.3 fusion.2
  69.8 0.1 copy.28
  69.9 0.3 copy.13
  70.2 5.1 %collective-permute-start.17 = (bf16[2,128,128]{2,1,0:T(8,128)(2,1)S(1)}, bf16[2,128,128]{2,1,0:T(8,128)(2,1)S(1)}, u32[]{:S(2)}, u32[]{:S(2)}) collective-permute-start(bf16[2,128,128]{2,1,0:T(8,128)(2,1)S(1)} %collective-permute-done.13), channel_id=1, source_target_pairs={{0,14},{2,0},{4,2},{6,4},{8,6},{10,8},{12,10},{14,12},{1,15},{3,1}... | collective-permute-start | bytes 196616 | tf_op jit(solution)/shard_map/ppermute | solution.py:20
  75.3 0.1 fusion.15
  75.5 0.1 copy.14
  75.6 1.6 %collective-permute-start.19 = (bf16[4,1,128,128]{3,2,0,1:T(8,128)(2,1)S(1)}, bf16[4,1,128,128]{3,2,0,1:T(8,128)(2,1)S(1)}, u32[]{:S(2)}, u32[]{:S(2)}) collective-permute-start(bf16[4,1,128,128]{3,2,0,1:T(8,128)(2,1)S(1)} %collective-permute-done.15), channel_id=1, source_target_pairs={{0,16},{16,0},{1,17},{17,1},{2,18},{18,2},{3,19},{19,3},{4,20},{20... | collective-permute-start | bytes 393224 | tf_op jit(solution)/shard_map/ppermute | solution.py:20
  77.2 0.3 convolution_add_fusion.1
  77.6 0.3 fusion.3
  77.9 0.1 copy.33
  78.0 0.3 copy.15
  78.3 2.4 %collective-permute-done.19 = bf16[4,1,128,128]{3,2,0,1:T(8,128)(2,1)S(1)} collective-permute-done((bf16[4,1,128,128]{3,2,0,1:T(8,128)(2,1)S(1)}, bf16[4,1,128,128]{3,2,0,1:T(8,128)(2,1)S(1)}, u32[]{:S(2)}, u32[]{:S(2)}) %collective-permute-start.19) | collective-permute-done | bytes 131104 | tf_op jit(solution)/shard_map/ppermute | solution.py:20
  80.7 0.1 fusion.16
  80.8 0.1 copy.16
  81.0 1.3 %convolution_add_fusion = f32[1024,256]{1,0:T(8,128)} fusion(f32[1024,256]{1,0:T(8,128)S(1)} %convolution_add_fusion.1, bf16[32,8,8,128]{3,2,1,0:T(8,128)(2,1)S(1)} %bitcast.147, bf16[32,8,2,128]{3,2,1,0:T(2,128)(2,1)S(1)} %bitcast.155), kind=kOutput, calls=%fused_computation.4 | convolution fusion | flops 134479872 | bytes 2752512 | tf_op jit(solution)/shard_map/dot_general | solution.py:70
  82.3 0.0 reduce-scatter.2.cloned.1.call-update
  82.3 7.8 %reduce-scatter.2.cloned.1.call-done = f32[512,256]{1,0:T(8,128)} async-done(((f32[1024,256]{1,0:T(8,128)}), f32[512,256]{1,0:T(8,128)}) %reduce-scatter.2.cloned.1.call-update) | async-done | bytes 524304 | tf_op jit(solution)/shard_map/reduce_scatter | solution.py:110
  (35 shorter events, 0.2 us)
Async XLA Ops:
  6.5 83.5 %reduce-scatter.2.cloned.1.call-start = ((), (), s32[]{:S(2)}) async-start(), calls=%async_computation.1 | async-start | bytes 1572864 | tf_op jit(solution)/shard_map/reduce_scatter | solution.py:110
  6.5 6.0 %copy-start.2 = (s32[1,1,2]{2,1,0:T(1,128)S(1)}, s32[1,1,2]{2,1,0:T(1,128)}, u32[]{:S(2)}) copy-start(s32[1,1,2]{2,1,0:T(1,128)} %param.5) | copy-start | bytes 28
  6.5 41.6 %collective-permute-start.3 = (bf16[2,128,128]{2,1,0:T(8,128)(2,1)}, bf16[2,128,128]{2,1,0:T(8,128)(2,1)S(1)}, u32[]{:S(2)}, u32[]{:S(2)}) collective-permute-start(bf16[2,128,128]{2,1,0:T(8,128)(2,1)} %bitcast.158), channel_id=1, source_target_pairs={{0,14},{2,0},{4,2},{6,4},{8,6},{10,8},{12,10},{14,12},{1,15},{3,1}... | collective-permute-start | bytes 196616 | tf_op jit(solution)/shard_map/ppermute | solution.py:20
  12.5 3.5 %collective-permute-start = (s32[2]{0:T(128)S(1)}, s32[2]{0:T(128)S(1)}, u32[]{:S(2)}, u32[]{:S(2)}) collective-permute-start(s32[2]{0:T(128)S(1)} %bitcast.162), channel_id=1, source_target_pairs={{0,14},{2,0},{4,2},{6,4},{8,6},{10,8},{12,10},{14,12},{1,15},{3,1}... | collective-permute-start | bytes 32 | tf_op jit(solution)/shard_map/ppermute | solution.py:20
  13.2 1.5 %copy-start.3 = (s32[4,1,1,1]{0,3,2,1:T(1,128)S(1)}, s32[4,1,1,1]{0,3,2,1:T(1,128)}, u32[]{:S(2)}) copy-start(s32[4,1,1,1]{0,3,2,1:T(1,128)} %param.7) | copy-start | bytes 52
  13.2 35.0 %collective-permute-start.7 = (bf16[4,1,128,128]{3,2,0,1:T(8,128)(2,1)}, bf16[4,1,128,128]{3,2,0,1:T(8,128)(2,1)S(1)}, u32[]{:S(2)}, u32[]{:S(2)}) collective-permute-start(bf16[4,1,128,128]{3,2,0,1:T(8,128)(2,1)} %bitcast.157), channel_id=1, source_target_pairs={{0,16},{16,0},{1,17},{17,1},{2,18},{18,2},{3,19},{19,3},{4,20},{20... | collective-permute-start | bytes 393224 | tf_op jit(solution)/shard_map/ppermute | solution.py:20
  14.7 4.9 %collective-permute-start.6 = (s32[4,1]{0,1:T(1,128)S(1)}, s32[4,1]{0,1:T(1,128)S(1)}, u32[]{:S(2)}, u32[]{:S(2)}) collective-permute-start(s32[4,1]{0,1:T(1,128)S(1)} %bitcast.163), channel_id=1, source_target_pairs={{0,16},{16,0},{1,17},{17,1},{2,18},{18,2},{3,19},{19,3},{4,20},{20... | collective-permute-start | bytes 56 | tf_op jit(solution)/shard_map/ppermute | solution.py:20
  15.3 32.8 %copy-start.1 = (bf16[1,1,2,128,128]{4,3,2,1,0:T(8,128)(2,1)S(1)}, bf16[1,1,2,128,128]{4,3,2,1,0:T(8,128)(2,1)}, u32[]{:S(2)}) copy-start(bf16[1,1,2,128,128]{4,3,2,1,0:T(8,128)(2,1)} %param.4) | copy-start | bytes 196612
  15.3 32.9 %copy-start = (bf16[4,1,1,1,128,128]{5,4,3,2,1,0:T(8,128)(2,1)S(1)}, bf16[4,1,1,1,128,128]{5,4,3,2,1,0:T(8,128)(2,1)}, u32[]{:S(2)}) copy-start(bf16[4,1,1,1,128,128]{5,4,3,2,1,0:T(8,128)(2,1)} %param.6) | copy-start | bytes 393220
  16.1 3.5 %collective-permute-start.1 = (s32[2]{0:T(128)S(1)}, s32[2]{0:T(128)S(1)}, u32[]{:S(2)}, u32[]{:S(2)}) collective-permute-start(s32[2]{0:T(128)S(1)} %broadcast_select_fusion.5), channel_id=1, source_target_pairs={{0,12},{2,14},{4,0},{6,2},{8,4},{10,6},{12,8},{14,10},{1,13},{3,15... | collective-permute-start | bytes 32 | tf_op jit(solution)/shard_map/ppermute | solution.py:20
  19.6 4.4 %collective-permute-start.2 = (s32[2]{0:T(128)S(1)}, s32[2]{0:T(128)S(1)}, u32[]{:S(2)}, u32[]{:S(2)}) collective-permute-start(s32[2]{0:T(128)S(1)} %broadcast_select_fusion.6), channel_id=1, source_target_pairs={{0,8},{2,10},{4,12},{6,14},{8,0},{10,2},{12,4},{14,6},{1,9},{3,11}... | collective-permute-start | bytes 32 | tf_op jit(solution)/shard_map/ppermute | solution.py:20
  19.6 9.9 %collective-permute-start.10 = (s32[4,1]{0,1:T(1,128)S(1)}, s32[4,1]{0,1:T(1,128)S(1)}, u32[]{:S(2)}, u32[]{:S(2)}) collective-permute-start(s32[4,1]{0,1:T(1,128)S(1)} %broadcast_select_fusion.4), channel_id=1, source_target_pairs={{0,16},{16,0},{1,17},{17,1},{2,18},{18,2},{3,19},{19,3},{4,20},{20... | collective-permute-start | bytes 56 | tf_op jit(solution)/shard_map/ppermute | solution.py:20
  24.1 8.3 %collective-permute-start.8 = (s32[2]{0:T(128)S(1)}, s32[2]{0:T(128)S(1)}, u32[]{:S(2)}, u32[]{:S(2)}) collective-permute-start(s32[2]{0:T(128)S(1)} %broadcast_select_fusion.7), channel_id=1, source_target_pairs={{0,14},{2,0},{4,2},{6,4},{8,6},{10,8},{12,10},{14,12},{1,15},{3,1}... | collective-permute-start | bytes 32 | tf_op jit(solution)/shard_map/ppermute | solution.py:20
  30.8 11.2 %collective-permute-start.14 = (s32[4,1]{0,1:T(1,128)S(1)}, s32[4,1]{0,1:T(1,128)S(1)}, u32[]{:S(2)}, u32[]{:S(2)}) collective-permute-start(s32[4,1]{0,1:T(1,128)S(1)} %collective-permute-done.10), channel_id=1, source_target_pairs={{0,16},{16,0},{1,17},{17,1},{2,18},{18,2},{3,19},{19,3},{4,20},{20... | collective-permute-start | bytes 56 | tf_op jit(solution)/shard_map/ppermute | solution.py:20
  32.4 4.7 %collective-permute-start.12 = (s32[2]{0:T(128)S(1)}, s32[2]{0:T(128)S(1)}, u32[]{:S(2)}, u32[]{:S(2)}) collective-permute-start(s32[2]{0:T(128)S(1)} %collective-permute-done.8), channel_id=1, source_target_pairs={{0,14},{2,0},{4,2},{6,4},{8,6},{10,8},{12,10},{14,12},{1,15},{3,1}... | collective-permute-start | bytes 32 | tf_op jit(solution)/shard_map/ppermute | solution.py:20
  37.1 40.5 %collective-permute-start.16 = (s32[2]{0:T(128)S(1)}, s32[2]{0:T(128)S(1)}, u32[]{:S(2)}, u32[]{:S(2)}) collective-permute-start(s32[2]{0:T(128)S(1)} %collective-permute-done.12), channel_id=1, source_target_pairs={{0,14},{2,0},{4,2},{6,4},{8,6},{10,8},{12,10},{14,12},{1,15},{3,1}... | collective-permute-start | bytes 32 | tf_op jit(solution)/shard_map/ppermute | solution.py:20
  43.3 3.6 %collective-permute-start.18 = (s32[4,1]{0,1:T(1,128)S(1)}, s32[4,1]{0,1:T(1,128)S(1)}, u32[]{:S(2)}, u32[]{:S(2)}) collective-permute-start(s32[4,1]{0,1:T(1,128)S(1)} %collective-permute-done.14), channel_id=1, source_target_pairs={{0,16},{16,0},{1,17},{17,1},{2,18},{18,2},{3,19},{19,3},{4,20},{20... | collective-permute-start | bytes 56 | tf_op jit(solution)/shard_map/ppermute | solution.py:20
  48.1 4.3 %collective-permute-start.4 = (bf16[2,128,128]{2,1,0:T(8,128)(2,1)S(1)}, bf16[2,128,128]{2,1,0:T(8,128)(2,1)S(1)}, u32[]{:S(2)}, u32[]{:S(2)}) collective-permute-start(bf16[2,128,128]{2,1,0:T(8,128)(2,1)S(1)} %broadcast_select_fusion.1), channel_id=1, source_target_pairs={{0,12},{2,14},{4,0},{6,2},{8,4},{10,6},{12,8},{14,10},{1,13},{3,15... | collective-permute-start | bytes 196616 | tf_op jit(solution)/shard_map/ppermute | solution.py:20
  48.3 15.2 %collective-permute-start.11 = (bf16[4,1,128,128]{3,2,0,1:T(8,128)(2,1)S(1)}, bf16[4,1,128,128]{3,2,0,1:T(8,128)(2,1)S(1)}, u32[]{:S(2)}, u32[]{:S(2)}) collective-permute-start(bf16[4,1,128,128]{3,2,0,1:T(8,128)(2,1)S(1)} %broadcast_select_fusion), channel_id=1, source_target_pairs={{0,16},{16,0},{1,17},{17,1},{2,18},{18,2},{3,19},{19,3},{4,20},{20... | collective-permute-start | bytes 393224 | tf_op jit(solution)/shard_map/ppermute | solution.py:20
  52.5 5.5 %collective-permute-start.5 = (bf16[2,128,128]{2,1,0:T(8,128)(2,1)S(1)}, bf16[2,128,128]{2,1,0:T(8,128)(2,1)S(1)}, u32[]{:S(2)}, u32[]{:S(2)}) collective-permute-start(bf16[2,128,128]{2,1,0:T(8,128)(2,1)S(1)} %broadcast_select_fusion.2), channel_id=1, source_target_pairs={{0,8},{2,10},{4,12},{6,14},{8,0},{10,2},{12,4},{14,6},{1,9},{3,11}... | collective-permute-start | bytes 196616 | tf_op jit(solution)/shard_map/ppermute | solution.py:20
  57.9 4.8 %collective-permute-start.9 = (bf16[2,128,128]{2,1,0:T(8,128)(2,1)S(1)}, bf16[2,128,128]{2,1,0:T(8,128)(2,1)S(1)}, u32[]{:S(2)}, u32[]{:S(2)}) collective-permute-start(bf16[2,128,128]{2,1,0:T(8,128)(2,1)S(1)} %broadcast_select_fusion.3), channel_id=1, source_target_pairs={{0,14},{2,0},{4,2},{6,4},{8,6},{10,8},{12,10},{14,12},{1,15},{3,1}... | collective-permute-start | bytes 196616 | tf_op jit(solution)/shard_map/ppermute | solution.py:20
  63.8 5.7 %collective-permute-start.13 = (bf16[2,128,128]{2,1,0:T(8,128)(2,1)S(1)}, bf16[2,128,128]{2,1,0:T(8,128)(2,1)S(1)}, u32[]{:S(2)}, u32[]{:S(2)}) collective-permute-start(bf16[2,128,128]{2,1,0:T(8,128)(2,1)S(1)} %collective-permute-done.9), channel_id=1, source_target_pairs={{0,14},{2,0},{4,2},{6,4},{8,6},{10,8},{12,10},{14,12},{1,15},{3,1}... | collective-permute-start | bytes 196616 | tf_op jit(solution)/shard_map/ppermute | solution.py:20
  67.6 7.7 %collective-permute-start.15 = (bf16[4,1,128,128]{3,2,0,1:T(8,128)(2,1)S(1)}, bf16[4,1,128,128]{3,2,0,1:T(8,128)(2,1)S(1)}, u32[]{:S(2)}, u32[]{:S(2)}) collective-permute-start(bf16[4,1,128,128]{3,2,0,1:T(8,128)(2,1)S(1)} %collective-permute-done.11), channel_id=1, source_target_pairs={{0,16},{16,0},{1,17},{17,1},{2,18},{18,2},{3,19},{19,3},{4,20},{20... | collective-permute-start | bytes 393224 | tf_op jit(solution)/shard_map/ppermute | solution.py:20
  70.2 7.4 %collective-permute-start.17 = (bf16[2,128,128]{2,1,0:T(8,128)(2,1)S(1)}, bf16[2,128,128]{2,1,0:T(8,128)(2,1)S(1)}, u32[]{:S(2)}, u32[]{:S(2)}) collective-permute-start(bf16[2,128,128]{2,1,0:T(8,128)(2,1)S(1)} %collective-permute-done.13), channel_id=1, source_target_pairs={{0,14},{2,0},{4,2},{6,4},{8,6},{10,8},{12,10},{14,12},{1,15},{3,1}... | collective-permute-start | bytes 196616 | tf_op jit(solution)/shard_map/ppermute | solution.py:20
  75.6 5.0 %collective-permute-start.19 = (bf16[4,1,128,128]{3,2,0,1:T(8,128)(2,1)S(1)}, bf16[4,1,128,128]{3,2,0,1:T(8,128)(2,1)S(1)}, u32[]{:S(2)}, u32[]{:S(2)}) collective-permute-start(bf16[4,1,128,128]{3,2,0,1:T(8,128)(2,1)S(1)} %collective-permute-done.15), channel_id=1, source_target_pairs={{0,16},{16,0},{1,17},{17,1},{2,18},{18,2},{3,19},{19,3},{4,20},{20... | collective-permute-start | bytes 393224 | tf_op jit(solution)/shard_map/ppermute | solution.py:20
Sparse Core Ops, SparseCore 0:
  82.4 7.5 reduce-scatter.1
where the time goes:
time: 97.1 us; the launch traced here: 96.9 us
  starting transfers between devices  43.2 us (44%)
  waiting for transfers between devices  28.7 us (30%)
  between operations  13.7 us (14%)
  local copies, waits for them, and re-layouts  4.57 us (5%)
  matrix products  3.51 us (4%)
  other arithmetic  3.16 us (3%)
    ppermute x20, starting transfers between devices, passed_along(): lax.ppermute(value, axis, [(i, (i + by) % count) for i in range(count)])  43.2 us
    ppermute x20, waiting for transfers between devices, passed_along(): lax.ppermute(value, axis, [(i, (i + by) % count) for i in range(count)])  21 us
    reduce_scatter x1, waiting for transfers between devices, per_device(): return lax.psum_scatter(total, 'layer', scatter_dimension=0, tiled=True)  7.76 us
    another operation x8, other arithmetic  2.63 us
    dot_general x4, matrix products, dense_kernel(): return total + jnp.dot(s_tile, x_tile, preferred_element_type=jnp.float32)  2.4 us
    dynamic_slice x4, local copies, waits for them, and re-layouts, per_device(): lax.dynamic_index_in_dim(held_x[1], group_pick, 0, keepdims=False)  2.32 us
  transfers between devices with their start and end apart: 21, of which 10 were waited for; matrix products, arithmetic and copies ran while one was open for 10% of the time, Pallas kernels for 0%

commit v1 on v0

v1 whole, which is shorter than its diff:
```python
import functools

import jax
import jax.numpy as jnp
from jax import lax
from jax.experimental import pallas as pl
from jax.experimental.pallas import tpu as pltpu
from jax.sharding import PartitionSpec as P

BR = 8
BC = 2
TAIL = 16


def pack_kernel(s_ref, s_slots_ref, x_ref, x_slots_ref, s_out, x_out, s_at, x_at, sems):
    block = s_out.shape[-1]
    moves = [(s_slots_ref, s_at), (x_slots_ref, x_at)]
    for ref, out in ((s_ref, s_out), (x_ref, x_out)):
        for at in range(0, ref.shape[0], block):
            rows = pl.ds(at, block)
            moves.append((ref.at[rows], out.at[rows]))
    copies = [pltpu.make_async_copy(*move, sems.at[at]) for at, move in enumerate(moves)]
    for copy in copies:
        copy.start()
    lane = lax.broadcasted_iota(jnp.int32, (TAIL, block), 1)
    for copy, slots, out in zip(copies, (s_at, x_at), (s_out, x_out)):
        copy.wait()
        tail = jnp.zeros(lane.shape, jnp.float32)
        for a in range(slots.shape[0]):
            tail = jnp.where(lane == a, slots[a].astype(jnp.float32), tail)
        out[out.shape[0] - TAIL :] = tail.astype(jnp.bfloat16)
    for copy in copies[2:]:
        copy.wait()


def slots_of(ref, count):
    tail = ref[ref.shape[0] - TAIL :].astype(jnp.float32)
    return [tail[0, a].astype(jnp.int32) for a in range(count)]


def swap_order(n_col):
    far = list(range(n_col - 2, n_col // 2 - 1, -2))
    return far[:1] + list(range(n_col // 2 - 2, 0, -2)) + far[1:]


def add_products(total, pieces, x_all, x_at, slots, inner):
    layer = lax.axis_index("layer")
    block = x_all.shape[-1]
    per_layer = total.shape[0] // block
    zero = jnp.zeros((block, block), jnp.bfloat16)
    s_at = [slots_of(ref, slots) for ref, _ in pieces]
    for first in range(0, len(pieces), 2):
        pair = pieces[first : first + 2]
        x0, x1 = [x_all[piece] for _, piece in pair]
        right = jnp.concatenate(
            [
                jnp.concatenate([x0, zero], axis=1),
                jnp.concatenate([zero, x1], axis=1),
            ],
            axis=0,
        )
        left = jnp.concatenate([ref[: slots * block] for ref, _ in pair], axis=1)
        tiles = jnp.dot(left, right, preferred_element_type=jnp.float32)
        for e, (_, piece) in enumerate(pair):
            x_slot = x_at[piece]
            columns = pl.ds(pl.multiple_of(x_slot % BC * block, block), block)
            for a, s_slot in enumerate(s_at[first + e]):
                at = s_slot // inner - layer * per_layer
                live = (at >= 0) & (at < per_layer) & (s_slot % inner == x_slot // BC)
                rows = pl.ds(pl.multiple_of(jnp.clip(at, 0, per_layer - 1) * block, block), block)
                tile = tiles[a * block : (a + 1) * block, e * block : (e + 1) * block]
                total[rows, columns] += jnp.where(live, tile, 0.0)


def early_kernel(sizes, *refs):
    n_row, n_col, inner, slots, q = sizes
    x_refs, s_refs = refs[:n_row], refs[n_row : n_row + n_col // 2]
    total, x_all, x_at = refs[n_row + n_col // 2 :]
    row, col, layer = lax.axis_index("row"), lax.axis_index("col"), lax.axis_index("layer")
    block = x_all.shape[-1]
    for k, ref in enumerate(x_refs):
        for m, slot in enumerate(slots_of(ref, q)):
            piece = m * n_row + (row ^ k)
            x_all[piece] = ref[m * block : (m + 1) * block]
            x_at[piece] = slot
    total[...] = jnp.zeros_like(total)
    masks = [0] + [mask + layer for mask in swap_order(n_col)]
    pieces = [(ref, col ^ mask) for ref, mask in zip(s_refs, masks)]
    add_products(total, pieces, x_all, x_at, slots, inner)


def final_kernel(sizes, x_at, x_all, total, *refs):
    n_row, n_col, inner, slots, q = sizes
    s_refs, out_ref = refs[:-1], refs[-1]
    col, layer = lax.axis_index("col"), lax.axis_index("layer")
    out_ref[...] = total[...]
    masks = [1] + [mask + 1 - layer for mask in swap_order(n_col)]
    pieces = [(ref, col ^ mask) for ref, mask in zip(s_refs, masks)]
    add_products(out_ref, pieces, x_all, x_at, slots, inner)


def swap(value, n_col, mask, other):
    pairs = []
    for c in range(n_col):
        pairs += [(c * 2, (c ^ mask) * 2), (c * 2 + 1, (c ^ other) * 2 + 1)]
    return lax.ppermute(value, ("col", "layer"), pairs)


def per_device(s_values, s_slots, x_values, x_slots):
    n_row = lax.axis_size("row")
    n_col = lax.axis_size("col")
    n_layer = lax.axis_size("layer")
    block = s_values.shape[-1]
    slots, q = s_values.shape[2], x_values.shape[0]
    arrays = (
        s_values.reshape(slots * block, block),
        s_slots.reshape(slots),
        x_values.reshape(q * block, block),
        x_slots.reshape(q),
    )
    s_piece, x_piece = pl.pallas_call(
        pack_kernel,
        out_shape=(
            pltpu.VMEM((slots * block + TAIL, block), jnp.bfloat16),
            pltpu.VMEM((q * block + TAIL, block), jnp.bfloat16),
        ),
        in_specs=[pl.BlockSpec(memory_space=pltpu.HBM)] * 4,
        out_specs=(pl.BlockSpec(memory_space=pltpu.VMEM),) * 2,
        scratch_shapes=[
            pltpu.SMEM((slots,), jnp.int32),
            pltpu.SMEM((q,), jnp.int32),
            pltpu.SemaphoreType.DMA((2 + slots + q,)),
        ],
        compiler_params=pltpu.CompilerParams(vmem_limit_bytes=4 << 20),
    )(*[pltpu.with_memory_space_constraint(array, pltpu.HBM) for array in arrays])
    order = swap_order(n_col)
    fetched = [swap(s_piece, n_col, mask, mask + 1) for mask in order]
    xs = [x_piece]
    for k in range(1, n_row):
        xs.append(lax.ppermute(x_piece, "row", [(i ^ k, i) for i in range(n_row)]))
    near = swap(s_piece, n_col, 1, 1)
    over = [(i, n_layer - 1 - i) for i in range(n_layer)]
    handed = [lax.ppermute(piece, "layer", over) for piece in fetched]
    smem, vmem = [pl.BlockSpec(memory_space=space) for space in (pltpu.SMEM, pltpu.VMEM)]
    params = pltpu.CompilerParams(vmem_limit_bytes=24 << 20)
    sizes = (n_row, n_col, n_row * BR // n_col, slots, q)
    shape = (BR // n_layer * block, BC * block)
    total, x_all, x_at = pl.pallas_call(
        functools.partial(early_kernel, sizes),
        out_shape=(
            pltpu.VMEM(shape, jnp.float32),
            pltpu.VMEM((q * n_row, block, block), jnp.bfloat16),
            pltpu.SMEM((q * n_row,), jnp.int32),
        ),
        in_specs=[vmem] * (n_row + 1 + len(fetched)),
        out_specs=(vmem, vmem, smem),
        compiler_params=params,
    )(*xs, s_piece, *fetched)
    return pl.pallas_call(
        functools.partial(final_kernel, sizes),
        out_shape=jax.ShapeDtypeStruct(shape, jnp.float32),
        in_specs=[smem] + [vmem] * (3 + len(handed)),
        out_specs=vmem,
        compiler_params=params,
    )(pltpu.with_memory_space_constraint(x_at, pltpu.SMEM), x_all, total, near, *handed)


def solution(mesh):
    placed = (
        P("row", "col", None, None, None),
        P("row", "col", None),
        P(None, "row", "col", None, None, None),
        P(None, "row", "col", None),
    )
    return jax.shard_map(
        per_device,
        mesh=mesh,
        in_specs=placed,
        out_specs=P(("row", "layer"), "col"),
        check_vma=False,
    )
```

time: 97.1 us -> 14.8 us (0.15)
  starting transfers between devices: 43.2 us -> 9.42 us
  waiting for transfers between devices: 28.7 us -> 2.87 us
  between operations: 13.7 us -> 0.05 us
  local copies, waits for them, and re-layouts: 4.57 us -> 0 us
  matrix products: 3.51 us -> 0 us
  other arithmetic: 3.16 us -> 0 us
  Pallas kernels: 0 us -> 2.32 us
    ppermute x20 -> x8, starting transfers between devices: 43.2 us -> 9.42 us  [the longest x4 7.25 us: swap(): return lax.ppermute(value, ('col', 'layer'), pairs)]
    ppermute x20 -> x8, waiting for transfers between devices: 21 us -> 2.87 us  [the longest x4 2.32 us: swap(): return lax.ppermute(value, ('col', 'layer'), pairs)]
    reduce_scatter x1 -> x0, waiting for transfers between devices: 7.76 us -> none  [per_device(): return lax.psum_scatter(total, 'layer', scatter_dimension=0, tiled=True)]
    dot_general x8 -> x0, matrix products: 3.51 us -> none  [the longest x4 2.4 us: dense_kernel(): return total + jnp.dot(s_tile, x_tile, preferred_element_type=jnp.float32)]
    another operation x8 -> x0, other arithmetic: 2.63 us -> none
    dynamic_slice x4 -> x0, local copies, waits for them, and re-layouts: 2.32 us -> none  [per_device(): lax.dynamic_index_in_dim(held_x[1], group_pick, 0, keepdims=False)]
    pallas_call x0 -> x3, Pallas kernels: none -> 2.32 us  [the longest x1 1.08 us: per_device(): pl.pallas_call(functools.partial(final_kernel, sizes), out_shape=jax.Shap...]
    reshape x4 -> x0, local copies, waits for them, and re-layouts: 1.24 us -> none  [dense_kernel(): tiles = flat.astype(jnp.bfloat16).reshape(BR, inner, block, block)]
  transfers between devices with their start and end apart: 21 -> 8, of which waited for: 10 -> 3; matrix products, arithmetic and copies ran while one was open for 10% -> 0% of each run, Pallas kernels for 0% -> 2%
where the time goes in v1:
time: 14.8 us; the launch traced here: 14.7 us
  starting transfers between devices  9.42 us (64%)
  waiting for transfers between devices  2.87 us (19%)
  Pallas kernels  2.32 us (16%)
    ppermute x4, starting transfers between devices, swap(): return lax.ppermute(value, ('col', 'layer'), pairs)  7.25 us
    ppermute x4, waiting for transfers between devices, swap(): return lax.ppermute(value, ('col', 'layer'), pairs)  2.32 us
    ppermute x1, starting transfers between devices, per_device(): xs.append(lax.ppermute(x_piece, 'row', [(i ^ k, i) for i in range(n_row)]))  1.66 us
    pallas_call x1, Pallas kernels, per_device(): pl.pallas_call(functools.partial(final_kernel, sizes), out_shape=jax.Shap...  1.08 us
    pallas_call x1, Pallas kernels, per_device(): pl.pallas_call(pack_kernel, out_shape=(pltpu.VMEM((slots * block + TAIL,...  0.91 us
    ppermute x3, starting transfers between devices, per_device(): handed = [lax.ppermute(piece, 'layer', over) for piece in fetched]  0.51 us
    ppermute x1, waiting for transfers between devices, per_device(): xs.append(lax.ppermute(x_piece, 'row', [(i ^ k, i) for i in range(n_row)]))  0.46 us
    pallas_call x1, Pallas kernels, per_device(): pl.pallas_call(functools.partial(early_kernel, sizes), out_shape=(pltpu.V...  0.33 us
  transfers between devices with their start and end apart: 8, of which 3 were waited for; matrix products, arithmetic and copies ran while one was open for 0% of the time, Pallas kernels for 2%

profile of v1, /device:TPU:0, one launch (start us, length us, event | category | flops | bytes accessed | tf_op | source)
XLA Modules:
  0.0 14.7 jit_solution(14986497662332131935)
XLA Ops:
  0.0 0.9 %shard_map.46 = (bf16[272,128]{1,0:T(8,128)(2,1)S(1)}, bf16[528,128]{1,0:T(8,128)(2,1)S(1)}) custom-call(bf16[256,128]{1,0:T(8,128)(2,1)} %bitcast.5, s32[2]{0:T(128)} %bitcast.6, bf16[512,128]{1,0:T(8,128)(2,1)} %bitcast.4, s32[4]{0:T(128)} %bitcast.7), custom_call_target="tpu_custom_call" | custom-call | tf_op jit(solution)/shard_map/pallas_call | solution.py:121
  0.9 5.1 %collective-permute-start.1 = (bf16[272,128]{1,0:T(8,128)(2,1)S(1)}, bf16[272,128]{1,0:T(8,128)(2,1)S(1)}, u32[]{:S(2)}, u32[]{:S(2)}) collective-permute-start(bf16[272,128]{1,0:T(8,128)(2,1)S(1)} %get-tuple-element.11.refs_2_), channel_id=1, source_target_pairs={{0,12},{1,15},{2,14},{3,13},{4,8},{5,11},{6,10},{7,9},{8,4},{9,7},... | collective-permute-start | bytes 208904 | tf_op jit(solution)/shard_map/ppermute | solution.py:106
  6.0 0.0 collective-permute-start.2
  6.0 0.6 %collective-permute-start.3 = (bf16[272,128]{1,0:T(8,128)(2,1)S(1)}, bf16[272,128]{1,0:T(8,128)(2,1)S(1)}, u32[]{:S(2)}, u32[]{:S(2)}) collective-permute-start(bf16[272,128]{1,0:T(8,128)(2,1)S(1)} %get-tuple-element.11.refs_2_), channel_id=1, source_target_pairs={{0,8},{1,11},{2,10},{3,9},{4,12},{5,15},{6,14},{7,13},{8,0},{9,3},... | collective-permute-start | bytes 208904 | tf_op jit(solution)/shard_map/ppermute | solution.py:106
  6.7 1.7 %collective-permute-start = (bf16[528,128]{1,0:T(8,128)(2,1)S(1)}, bf16[528,128]{1,0:T(8,128)(2,1)S(1)}, u32[]{:S(2)}, u32[]{:S(2)}) collective-permute-start(bf16[528,128]{1,0:T(8,128)(2,1)S(1)} %get-tuple-element.10.refs_0_), channel_id=1, source_target_pairs={{16,0},{0,16},{17,1},{1,17},{18,2},{2,18},{19,3},{3,19},{20,4},{4,... | collective-permute-start | bytes 405512 | tf_op jit(solution)/shard_map/ppermute | solution.py:140
  8.3 1.5 %collective-permute-start.4 = (bf16[272,128]{1,0:T(8,128)(2,1)S(1)}, bf16[272,128]{1,0:T(8,128)(2,1)S(1)}, u32[]{:S(2)}, u32[]{:S(2)}) collective-permute-start(bf16[272,128]{1,0:T(8,128)(2,1)S(1)} %get-tuple-element.11.refs_2_), channel_id=1, source_target_pairs={{0,2},{1,3},{2,0},{3,1},{4,6},{5,7},{6,4},{7,5},{8,10},{9,11},{10,... | collective-permute-start | bytes 208904 | tf_op jit(solution)/shard_map/ppermute | solution.py:106
  9.8 0.0 collective-permute-done.1.refs_3_
  9.8 0.0 collective-permute-start.5
  9.8 2.3 %collective-permute-done.2.refs_4_ = bf16[272,128]{1,0:T(8,128)(2,1)S(1)} collective-permute-done((bf16[272,128]{1,0:T(8,128)(2,1)S(1)}, bf16[272,128]{1,0:T(8,128)(2,1)S(1)}, u32[]{:S(2)}, u32[]{:S(2)}) %collective-permute-start.2) | collective-permute-done | bytes 69664 | tf_op jit(solution)/shard_map/ppermute | solution.py:106
  12.2 0.0 collective-permute-start.6
  12.2 0.0 collective-permute-done.3.refs_5_
  12.2 0.5 %collective-permute-start.7 = (bf16[272,128]{1,0:T(8,128)(2,1)S(1)}, bf16[272,128]{1,0:T(8,128)(2,1)S(1)}, u32[]{:S(2)}, u32[]{:S(2)}) collective-permute-start(bf16[272,128]{1,0:T(8,128)(2,1)S(1)} %collective-permute-done.3.refs_5_), channel_id=1, source_target_pairs={{0,1},{1,0},{2,3},{3,2},{4,5},{5,4},{6,7},{7,6},{8,9},{9,8},{10,11... | collective-permute-start | bytes 208904 | tf_op jit(solution)/shard_map/ppermute | solution.py:143
  12.7 0.5 %collective-permute-done.refs_1_ = bf16[528,128]{1,0:T(8,128)(2,1)S(1)} collective-permute-done((bf16[528,128]{1,0:T(8,128)(2,1)S(1)}, bf16[528,128]{1,0:T(8,128)(2,1)S(1)}, u32[]{:S(2)}, u32[]{:S(2)}) %collective-permute-start) | collective-permute-done | bytes 135200 | tf_op jit(solution)/shard_map/ppermute | solution.py:140
  13.1 0.3 %shard_map.47 = (f32[512,256]{1,0:T(8,128)S(1)}, bf16[8,128,128]{2,1,0:T(8,128)(2,1)S(1)}, s32[8]{0:T(128)S(4)}) custom-call(bf16[528,128]{1,0:T(8,128)(2,1)S(1)} %get-tuple-element.10.refs_0_, bf16[528,128]{1,0:T(8,128)(2,1)S(1)} %collective-permute-done.refs_1_, bf16[272,128]{1,0:T(8,128)(2,1)S(1)} %get-tuple-element.11.refs_2_, ...), custom_call_target="tpu_custom_call" | custom-call | tf_op jit(solution)/shard_map/pallas_call | solution.py:148
  13.5 0.0 collective-permute-done.4.refs_0_
  13.5 0.0 collective-permute-done.5.refs_1_
  13.5 0.0 collective-permute-done.6.refs_2_
  13.5 0.1 collective-permute-done.7.refs_3_
  13.6 1.1 %shard_map.48 = f32[512,256]{1,0:T(8,128)} custom-call(s32[8]{0:T(128)S(4)} %get-tuple-element.12.x_at, bf16[8,128,128]{2,1,0:T(8,128)(2,1)S(1)} %get-tuple-element.13.x_all, f32[512,256]{1,0:T(8,128)S(1)} %get-tuple-element.14.total, bf16[272,128]{1,0:T(8,128)(2,1)S(1)} %collective-permute-done.4.refs_0_, ...), custom_call_target="tpu_custom_call" | custom-call | tf_op jit(solution)/shard_map/pallas_call | solution.py:159
Async XLA Ops:
  0.9 8.9 %collective-permute-start.1 = (bf16[272,128]{1,0:T(8,128)(2,1)S(1)}, bf16[272,128]{1,0:T(8,128)(2,1)S(1)}, u32[]{:S(2)}, u32[]{:S(2)}) collective-permute-start(bf16[272,128]{1,0:T(8,128)(2,1)S(1)} %get-tuple-element.11.refs_2_), channel_id=1, source_target_pairs={{0,12},{1,15},{2,14},{3,13},{4,8},{5,11},{6,10},{7,9},{8,4},{9,7},... | collective-permute-start | bytes 208904 | tf_op jit(solution)/shard_map/ppermute | solution.py:106
  6.0 6.1 %collective-permute-start.2 = (bf16[272,128]{1,0:T(8,128)(2,1)S(1)}, bf16[272,128]{1,0:T(8,128)(2,1)S(1)}, u32[]{:S(2)}, u32[]{:S(2)}) collective-permute-start(bf16[272,128]{1,0:T(8,128)(2,1)S(1)} %get-tuple-element.11.refs_2_), channel_id=1, source_target_pairs={{0,4},{1,7},{2,6},{3,5},{4,0},{5,3},{6,2},{7,1},{8,12},{9,15},{10,... | collective-permute-start | bytes 208904 | tf_op jit(solution)/shard_map/ppermute | solution.py:106
  6.0 6.1 %collective-permute-start.3 = (bf16[272,128]{1,0:T(8,128)(2,1)S(1)}, bf16[272,128]{1,0:T(8,128)(2,1)S(1)}, u32[]{:S(2)}, u32[]{:S(2)}) collective-permute-start(bf16[272,128]{1,0:T(8,128)(2,1)S(1)} %get-tuple-element.11.refs_2_), channel_id=1, source_target_pairs={{0,8},{1,11},{2,10},{3,9},{4,12},{5,15},{6,14},{7,13},{8,0},{9,3},... | collective-permute-start | bytes 208904 | tf_op jit(solution)/shard_map/ppermute | solution.py:106
  6.7 6.5 %collective-permute-start = (bf16[528,128]{1,0:T(8,128)(2,1)S(1)}, bf16[528,128]{1,0:T(8,128)(2,1)S(1)}, u32[]{:S(2)}, u32[]{:S(2)}) collective-permute-start(bf16[528,128]{1,0:T(8,128)(2,1)S(1)} %get-tuple-element.10.refs_0_), channel_id=1, source_target_pairs={{16,0},{0,16},{17,1},{1,17},{18,2},{2,18},{19,3},{3,19},{20,4},{4,... | collective-permute-start | bytes 405512 | tf_op jit(solution)/shard_map/ppermute | solution.py:140
  8.3 5.1 %collective-permute-start.4 = (bf16[272,128]{1,0:T(8,128)(2,1)S(1)}, bf16[272,128]{1,0:T(8,128)(2,1)S(1)}, u32[]{:S(2)}, u32[]{:S(2)}) collective-permute-start(bf16[272,128]{1,0:T(8,128)(2,1)S(1)} %get-tuple-element.11.refs_2_), channel_id=1, source_target_pairs={{0,2},{1,3},{2,0},{3,1},{4,6},{5,7},{6,4},{7,5},{8,10},{9,11},{10,... | collective-permute-start | bytes 208904 | tf_op jit(solution)/shard_map/ppermute | solution.py:106
  9.8 3.6 %collective-permute-start.5 = (bf16[272,128]{1,0:T(8,128)(2,1)S(1)}, bf16[272,128]{1,0:T(8,128)(2,1)S(1)}, u32[]{:S(2)}, u32[]{:S(2)}) collective-permute-start(bf16[272,128]{1,0:T(8,128)(2,1)S(1)} %collective-permute-done.1.refs_3_), channel_id=1, source_target_pairs={{0,1},{1,0},{2,3},{3,2},{4,5},{5,4},{6,7},{7,6},{8,9},{9,8},{10,11... | collective-permute-start | bytes 208904 | tf_op jit(solution)/shard_map/ppermute | solution.py:143
  12.2 1.3 %collective-permute-start.6 = (bf16[272,128]{1,0:T(8,128)(2,1)S(1)}, bf16[272,128]{1,0:T(8,128)(2,1)S(1)}, u32[]{:S(2)}, u32[]{:S(2)}) collective-permute-start(bf16[272,128]{1,0:T(8,128)(2,1)S(1)} %collective-permute-done.2.refs_4_), channel_id=1, source_target_pairs={{0,1},{1,0},{2,3},{3,2},{4,5},{5,4},{6,7},{7,6},{8,9},{9,8},{10,11... | collective-permute-start | bytes 208904 | tf_op jit(solution)/shard_map/ppermute | solution.py:143
  12.2 1.4 %collective-permute-start.7 = (bf16[272,128]{1,0:T(8,128)(2,1)S(1)}, bf16[272,128]{1,0:T(8,128)(2,1)S(1)}, u32[]{:S(2)}, u32[]{:S(2)}) collective-permute-start(bf16[272,128]{1,0:T(8,128)(2,1)S(1)} %collective-permute-done.3.refs_5_), channel_id=1, source_target_pairs={{0,1},{1,0},{2,3},{3,2},{4,5},{5,4},{6,7},{7,6},{8,9},{9,8},{10,11... | collective-permute-start | bytes 208904 | tf_op jit(solution)/shard_map/ppermute | solution.py:143

commit v2 on v1

--- a/solution.py
+++ b/solution.py
@@ -12,18 +12,17 @@
 TAIL = 16
 
 
-def pack_kernel(s_ref, s_slots_ref, x_ref, x_slots_ref, s_out, x_out, s_at, x_at, sems):
+def pack_kernel(s_ref, s_slots_ref, x_slots_ref, s_out, x_tail_out, s_at, x_at, sems):
     block = s_out.shape[-1]
     moves = [(s_slots_ref, s_at), (x_slots_ref, x_at)]
-    for ref, out in ((s_ref, s_out), (x_ref, x_out)):
-        for at in range(0, ref.shape[0], block):
-            rows = pl.ds(at, block)
-            moves.append((ref.at[rows], out.at[rows]))
+    for at in range(0, s_ref.shape[0], block):
+        rows = pl.ds(at, block)
+        moves.append((s_ref.at[rows], s_out.at[rows]))
     copies = [pltpu.make_async_copy(*move, sems.at[at]) for at, move in enumerate(moves)]
     for copy in copies:
         copy.start()
     lane = lax.broadcasted_iota(jnp.int32, (TAIL, block), 1)
-    for copy, slots, out in zip(copies, (s_at, x_at), (s_out, x_out)):
+    for copy, slots, out in zip(copies, (s_at, x_at), (s_out, x_tail_out)):
         copy.wait()
         tail = jnp.zeros(lane.shape, jnp.float32)
         for a in range(slots.shape[0]):
@@ -33,14 +32,21 @@
         copy.wait()
 
 
+def join_kernel(x_ref, tail_ref, x_out):
+    rows = x_ref.shape[0]
+    x_out[:rows] = x_ref[...]
+    x_out[rows:] = tail_ref[...]
+
+
 def slots_of(ref, count):
     tail = ref[ref.shape[0] - TAIL :].astype(jnp.float32)
     return [tail[0, a].astype(jnp.int32) for a in range(count)]
 
 
 def swap_order(n_col):
-    far = list(range(n_col - 2, n_col // 2 - 1, -2))
-    return far[:1] + list(range(n_col // 2 - 2, 0, -2)) + far[1:]
+    if n_col == 8:
+        return [(6, 7), (2, 5), (4, 3)]
+    return [(mask, mask + 1) for mask in range(n_col - 2, 0, -2)]
 
 
 def add_products(total, pieces, x_all, x_at, slots, inner):
@@ -84,7 +90,7 @@
             x_all[piece] = ref[m * block : (m + 1) * block]
             x_at[piece] = slot
     total[...] = jnp.zeros_like(total)
-    masks = [0] + [mask + layer for mask in swap_order(n_col)]
+    masks = [0] + [one + layer * (two - one) for one, two in swap_order(n_col)]
     pieces = [(ref, col ^ mask) for ref, mask in zip(s_refs, masks)]
     add_products(total, pieces, x_all, x_at, slots, inner)
 
@@ -94,7 +100,7 @@
     s_refs, out_ref = refs[:-1], refs[-1]
     col, layer = lax.axis_index("col"), lax.axis_index("layer")
     out_ref[...] = total[...]
-    masks = [1] + [mask + 1 - layer for mask in swap_order(n_col)]
+    masks = [1] + [two + layer * (one - two) for one, two in swap_order(n_col)]
     pieces = [(ref, col ^ mask) for ref, mask in zip(s_refs, masks)]
     add_products(out_ref, pieces, x_all, x_at, slots, inner)
 
@@ -112,29 +118,35 @@
     n_layer = lax.axis_size("layer")
     block = s_values.shape[-1]
     slots, q = s_values.shape[2], x_values.shape[0]
-    arrays = (
-        s_values.reshape(slots * block, block),
-        s_slots.reshape(slots),
-        x_values.reshape(q * block, block),
-        x_slots.reshape(q),
-    )
-    s_piece, x_piece = pl.pallas_call(
+    hbm, vmem = [pl.BlockSpec(memory_space=space) for space in (pltpu.HBM, pltpu.VMEM)]
+    params = pltpu.CompilerParams(vmem_limit_bytes=4 << 20)
+    arrays = s_values.reshape(slots * block, block), s_slots.reshape(slots), x_slots.reshape(q)
+    s_piece, x_tail = pl.pallas_call(
         pack_kernel,
         out_shape=(
             pltpu.VMEM((slots * block + TAIL, block), jnp.bfloat16),
-            pltpu.VMEM((q * block + TAIL, block), jnp.bfloat16),
+            pltpu.VMEM((TAIL, block), jnp.bfloat16),
         ),
-        in_specs=[pl.BlockSpec(memory_space=pltpu.HBM)] * 4,
-        out_specs=(pl.BlockSpec(memory_space=pltpu.VMEM),) * 2,
+        in_specs=[hbm] * len(arrays),
+        out_specs=(vmem, vmem),
         scratch_shapes=[
             pltpu.SMEM((slots,), jnp.int32),
             pltpu.SMEM((q,), jnp.int32),
-            pltpu.SemaphoreType.DMA((2 + slots + q,)),
+            pltpu.SemaphoreType.DMA((2 + slots,)),
         ],
-        compiler_params=pltpu.CompilerParams(vmem_limit_bytes=4 << 20),
+        compiler_params=params,
+        cost_estimate=pl.CostEstimate(flops=1_000_000_000, bytes_accessed=1_000_000, transcendentals=0),
     )(*[pltpu.with_memory_space_constraint(array, pltpu.HBM) for array in arrays])
+    x_blocks = pltpu.with_memory_space_constraint(x_values.reshape(q * block, block), pltpu.VMEM)
+    x_piece = pl.pallas_call(
+        join_kernel,
+        out_shape=pltpu.VMEM((q * block + TAIL, block), jnp.bfloat16),
+        in_specs=[vmem] * 2,
+        out_specs=vmem,
+        compiler_params=params,
+    )(x_blocks, x_tail)
     order = swap_order(n_col)
-    fetched = [swap(s_piece, n_col, mask, mask + 1) for mask in order]
+    fetched = [swap(s_piece, n_col, *masks) for masks in order]
     xs = [x_piece]
     for k in range(1, n_row):
         xs.append(lax.ppermute(x_piece, "row", [(i ^ k, i) for i in range(n_row)]))

time: 14.8 us -> 14.8 us (level)
  no operation moved by 1% of the time
where the time goes in v2:
time: 14.8 us; the launch traced here: 14.6 us
  starting transfers between devices  9.35 us (63%)
  waiting for transfers between devices  2.93 us (20%)
  Pallas kernels  2.28 us (15%)
    ppermute x4, starting transfers between devices, swap(): return lax.ppermute(value, ('col', 'layer'), pairs)  7.25 us
    ppermute x4, waiting for transfers between devices, swap(): return lax.ppermute(value, ('col', 'layer'), pairs)  2.38 us
    ppermute x1, starting transfers between devices, per_device(): xs.append(lax.ppermute(x_piece, 'row', [(i ^ k, i) for i in range(n_row)]))  1.73 us
    pallas_call x1, Pallas kernels, per_device(): pl.pallas_call(functools.partial(final_kernel, sizes), out_shape=jax.Shap...  1.09 us
    pallas_call x1, Pallas kernels, per_device(): pl.pallas_call(pack_kernel, out_shape=(pltpu.VMEM((slots * block + TAIL,...  0.86 us
    ppermute x1, waiting for transfers between devices, per_device(): xs.append(lax.ppermute(x_piece, 'row', [(i ^ k, i) for i in range(n_row)]))  0.55 us
    ppermute x3, starting transfers between devices, per_device(): handed = [lax.ppermute(piece, 'layer', over) for piece in fetched]  0.37 us
    pallas_call x1, Pallas kernels, per_device(): pl.pallas_call(functools.partial(early_kernel, sizes), out_shape=(pltpu.V...  0.32 us
  transfers between devices with their start and end apart: 8, of which 3 were waited for; matrix products, arithmetic and copies ran while one was open for 0% of the time, Pallas kernels for 2%

profile of v2, /device:TPU:0, one launch (start us, length us, event | category | flops | bytes accessed | tf_op | source)
XLA Modules:
  0.0 14.6 jit_solution(9677628106217905676)
XLA Ops:
  0.0 0.0 copy-start
  0.0 0.9 %shard_map.46 = (bf16[272,128]{1,0:T(8,128)(2,1)S(1)}, bf16[16,128]{1,0:T(8,128)(2,1)S(1)}) custom-call(bf16[256,128]{1,0:T(8,128)(2,1)} %bitcast.5, s32[2]{0:T(128)} %bitcast.6, s32[4]{0:T(128)} %bitcast.7), custom_call_target="tpu_custom_call" | custom-call | flops 1000000000 | bytes 1000000 | tf_op jit(solution)/shard_map/pallas_call | solution.py:124
  0.9 5.1 %collective-permute-start.1 = (bf16[272,128]{1,0:T(8,128)(2,1)S(1)}, bf16[272,128]{1,0:T(8,128)(2,1)S(1)}, u32[]{:S(2)}, u32[]{:S(2)}) collective-permute-start(bf16[272,128]{1,0:T(8,128)(2,1)S(1)} %get-tuple-element.11.refs_2_), channel_id=1, source_target_pairs={{0,12},{1,15},{2,14},{3,13},{4,8},{5,11},{6,10},{7,9},{8,4},{9,7},... | collective-permute-start | bytes 208904 | tf_op jit(solution)/shard_map/ppermute | solution.py:112
  6.0 0.0 collective-permute-start.2
  6.0 0.6 %collective-permute-start.3 = (bf16[272,128]{1,0:T(8,128)(2,1)S(1)}, bf16[272,128]{1,0:T(8,128)(2,1)S(1)}, u32[]{:S(2)}, u32[]{:S(2)}) collective-permute-start(bf16[272,128]{1,0:T(8,128)(2,1)S(1)} %get-tuple-element.11.refs_2_), channel_id=1, source_target_pairs={{0,8},{1,7},{2,10},{3,5},{4,12},{5,3},{6,14},{7,1},{8,0},{9,15},{1... | collective-permute-start | bytes 208904 | tf_op jit(solution)/shard_map/ppermute | solution.py:112
  6.6 0.0 copy-done
  6.6 1.7 %collective-permute-start = (bf16[528,128]{1,0:T(8,128)(2,1)S(1)}, bf16[528,128]{1,0:T(8,128)(2,1)S(1)}, u32[]{:S(2)}, u32[]{:S(2)}) collective-permute-start(bf16[528,128]{1,0:T(8,128)(2,1)S(1)} %shard_map.47.refs_0_), channel_id=1, source_target_pairs={{16,0},{0,16},{17,1},{1,17},{18,2},{2,18},{19,3},{3,19},{20,4},{4,... | collective-permute-start | bytes 405512 | tf_op jit(solution)/shard_map/ppermute | solution.py:152
  8.4 1.5 %collective-permute-start.4 = (bf16[272,128]{1,0:T(8,128)(2,1)S(1)}, bf16[272,128]{1,0:T(8,128)(2,1)S(1)}, u32[]{:S(2)}, u32[]{:S(2)}) collective-permute-start(bf16[272,128]{1,0:T(8,128)(2,1)S(1)} %get-tuple-element.11.refs_2_), channel_id=1, source_target_pairs={{0,2},{1,3},{2,0},{3,1},{4,6},{5,7},{6,4},{7,5},{8,10},{9,11},{10,... | collective-permute-start | bytes 208904 | tf_op jit(solution)/shard_map/ppermute | solution.py:112
  9.9 0.0 collective-permute-done.1.refs_3_
  9.9 0.0 collective-permute-start.5
  9.9 2.2 %collective-permute-done.2.refs_4_ = bf16[272,128]{1,0:T(8,128)(2,1)S(1)} collective-permute-done((bf16[272,128]{1,0:T(8,128)(2,1)S(1)}, bf16[272,128]{1,0:T(8,128)(2,1)S(1)}, u32[]{:S(2)}, u32[]{:S(2)}) %collective-permute-start.2) | collective-permute-done | bytes 69664 | tf_op jit(solution)/shard_map/ppermute | solution.py:112
  12.1 0.0 collective-permute-start.6
  12.1 0.1 collective-permute-done.3.refs_5_
  12.2 0.4 %collective-permute-start.7 = (bf16[272,128]{1,0:T(8,128)(2,1)S(1)}, bf16[272,128]{1,0:T(8,128)(2,1)S(1)}, u32[]{:S(2)}, u32[]{:S(2)}) collective-permute-start(bf16[272,128]{1,0:T(8,128)(2,1)S(1)} %collective-permute-done.3.refs_5_), channel_id=1, source_target_pairs={{0,1},{1,0},{2,3},{3,2},{4,5},{5,4},{6,7},{7,6},{8,9},{9,8},{10,11... | collective-permute-start | bytes 208904 | tf_op jit(solution)/shard_map/ppermute | solution.py:155
  12.6 0.5 %collective-permute-done.refs_1_ = bf16[528,128]{1,0:T(8,128)(2,1)S(1)} collective-permute-done((bf16[528,128]{1,0:T(8,128)(2,1)S(1)}, bf16[528,128]{1,0:T(8,128)(2,1)S(1)}, u32[]{:S(2)}, u32[]{:S(2)}) %collective-permute-start) | collective-permute-done | bytes 135200 | tf_op jit(solution)/shard_map/ppermute | solution.py:152
  13.2 0.3 %shard_map.48 = (f32[512,256]{1,0:T(8,128)S(1)}, bf16[8,128,128]{2,1,0:T(8,128)(2,1)S(1)}, s32[8]{0:T(128)S(4)}) custom-call(bf16[528,128]{1,0:T(8,128)(2,1)S(1)} %shard_map.47.refs_0_, bf16[528,128]{1,0:T(8,128)(2,1)S(1)} %collective-permute-done.refs_1_, bf16[272,128]{1,0:T(8,128)(2,1)S(1)} %get-tuple-element.11.refs_2_, ...), custom_call_target="tpu_custom_call" | custom-call | tf_op jit(solution)/shard_map/pallas_call | solution.py:160
  13.5 0.0 collective-permute-done.4.refs_0_
  13.5 0.0 collective-permute-done.5.refs_1_
  13.5 0.0 collective-permute-done.6.refs_2_
  13.5 0.0 collective-permute-done.7.refs_3_
  13.5 1.1 %shard_map.49 = f32[512,256]{1,0:T(8,128)} custom-call(s32[8]{0:T(128)S(4)} %get-tuple-element.12.x_at, bf16[8,128,128]{2,1,0:T(8,128)(2,1)S(1)} %get-tuple-element.13.x_all, f32[512,256]{1,0:T(8,128)S(1)} %get-tuple-element.14.total, bf16[272,128]{1,0:T(8,128)(2,1)S(1)} %collective-permute-done.4.refs_0_, ...), custom_call_target="tpu_custom_call" | custom-call | tf_op jit(solution)/shard_map/pallas_call | solution.py:171
  (1 shorter events, 0.0 us)
Async XLA Ops:
  0.0 6.6 %copy-start = (bf16[4,1,1,1,128,128]{5,4,3,2,1,0:T(8,128)(2,1)S(1)}, bf16[4,1,1,1,128,128]{5,4,3,2,1,0:T(8,128)(2,1)}, u32[]{:S(2)}) copy-start(bf16[4,1,1,1,128,128]{5,4,3,2,1,0:T(8,128)(2,1)} %param.6) | copy-start | bytes 393220
  0.9 9.0 %collective-permute-start.1 = (bf16[272,128]{1,0:T(8,128)(2,1)S(1)}, bf16[272,128]{1,0:T(8,128)(2,1)S(1)}, u32[]{:S(2)}, u32[]{:S(2)}) collective-permute-start(bf16[272,128]{1,0:T(8,128)(2,1)S(1)} %get-tuple-element.11.refs_2_), channel_id=1, source_target_pairs={{0,12},{1,15},{2,14},{3,13},{4,8},{5,11},{6,10},{7,9},{8,4},{9,7},... | collective-permute-start | bytes 208904 | tf_op jit(solution)/shard_map/ppermute | solution.py:112
  6.0 6.1 %collective-permute-start.2 = (bf16[272,128]{1,0:T(8,128)(2,1)S(1)}, bf16[272,128]{1,0:T(8,128)(2,1)S(1)}, u32[]{:S(2)}, u32[]{:S(2)}) collective-permute-start(bf16[272,128]{1,0:T(8,128)(2,1)S(1)} %get-tuple-element.11.refs_2_), channel_id=1, source_target_pairs={{0,4},{1,11},{2,6},{3,9},{4,0},{5,15},{6,2},{7,13},{8,12},{9,3},{1... | collective-permute-start | bytes 208904 | tf_op jit(solution)/shard_map/ppermute | solution.py:112
  6.0 6.3 %collective-permute-start.3 = (bf16[272,128]{1,0:T(8,128)(2,1)S(1)}, bf16[272,128]{1,0:T(8,128)(2,1)S(1)}, u32[]{:S(2)}, u32[]{:S(2)}) collective-permute-start(bf16[272,128]{1,0:T(8,128)(2,1)S(1)} %get-tuple-element.11.refs_2_), channel_id=1, source_target_pairs={{0,8},{1,7},{2,10},{3,5},{4,12},{5,3},{6,14},{7,1},{8,0},{9,15},{1... | collective-permute-start | bytes 208904 | tf_op jit(solution)/shard_map/ppermute | solution.py:112
  6.6 6.5 %collective-permute-start = (bf16[528,128]{1,0:T(8,128)(2,1)S(1)}, bf16[528,128]{1,0:T(8,128)(2,1)S(1)}, u32[]{:S(2)}, u32[]{:S(2)}) collective-permute-start(bf16[528,128]{1,0:T(8,128)(2,1)S(1)} %shard_map.47.refs_0_), channel_id=1, source_target_pairs={{16,0},{0,16},{17,1},{1,17},{18,2},{2,18},{19,3},{3,19},{20,4},{4,... | collective-permute-start | bytes 405512 | tf_op jit(solution)/shard_map/ppermute | solution.py:152
  8.4 5.1 %collective-permute-start.4 = (bf16[272,128]{1,0:T(8,128)(2,1)S(1)}, bf16[272,128]{1,0:T(8,128)(2,1)S(1)}, u32[]{:S(2)}, u32[]{:S(2)}) collective-permute-start(bf16[272,128]{1,0:T(8,128)(2,1)S(1)} %get-tuple-element.11.refs_2_), channel_id=1, source_target_pairs={{0,2},{1,3},{2,0},{3,1},{4,6},{5,7},{6,4},{7,5},{8,10},{9,11},{10,... | collective-permute-start | bytes 208904 | tf_op jit(solution)/shard_map/ppermute | solution.py:112
  9.9 3.6 %collective-permute-start.5 = (bf16[272,128]{1,0:T(8,128)(2,1)S(1)}, bf16[272,128]{1,0:T(8,128)(2,1)S(1)}, u32[]{:S(2)}, u32[]{:S(2)}) collective-permute-start(bf16[272,128]{1,0:T(8,128)(2,1)S(1)} %collective-permute-done.1.refs_3_), channel_id=1, source_target_pairs={{0,1},{1,0},{2,3},{3,2},{4,5},{5,4},{6,7},{7,6},{8,9},{9,8},{10,11... | collective-permute-start | bytes 208904 | tf_op jit(solution)/shard_map/ppermute | solution.py:155
  12.1 1.4 %collective-permute-start.6 = (bf16[272,128]{1,0:T(8,128)(2,1)S(1)}, bf16[272,128]{1,0:T(8,128)(2,1)S(1)}, u32[]{:S(2)}, u32[]{:S(2)}) collective-permute-start(bf16[272,128]{1,0:T(8,128)(2,1)S(1)} %collective-permute-done.2.refs_4_), channel_id=1, source_target_pairs={{0,1},{1,0},{2,3},{3,2},{4,5},{5,4},{6,7},{7,6},{8,9},{9,8},{10,11... | collective-permute-start | bytes 208904 | tf_op jit(solution)/shard_map/ppermute | solution.py:155
  12.2 1.3 %collective-permute-start.7 = (bf16[272,128]{1,0:T(8,128)(2,1)S(1)}, bf16[272,128]{1,0:T(8,128)(2,1)S(1)}, u32[]{:S(2)}, u32[]{:S(2)}) collective-permute-start(bf16[272,128]{1,0:T(8,128)(2,1)S(1)} %collective-permute-done.3.refs_5_), channel_id=1, source_target_pairs={{0,1},{1,0},{2,3},{3,2},{4,5},{5,4},{6,7},{7,6},{8,9},{9,8},{10,11... | collective-permute-start | bytes 208904 | tf_op jit(solution)/shard_map/ppermute | solution.py:155

commit v3 on v2

--- a/solution.py
+++ b/solution.py
@@ -45,7 +45,7 @@
 
 def swap_order(n_col):
     if n_col == 8:
-        return [(6, 7), (2, 5), (4, 3)]
+        return [(6, 7), (2, 4), (5, 3)]
     return [(mask, mask + 1) for mask in range(n_col - 2, 0, -2)]
 
 

time: 14.8 us -> 14.9 us (level)
  waiting for transfers between devices: 2.93 us -> 3.28 us
  starting transfers between devices: 9.35 us -> 9.11 us
    ppermute x4, waiting for transfers between devices: 2.38 us -> 2.92 us  [swap(): return lax.ppermute(value, ('col', 'layer'), pairs)]
    ppermute x3, starting transfers between devices: 0.37 us -> 0.16 us  [per_device(): handed = [lax.ppermute(piece, 'layer', over) for piece in fetched]]
    ppermute x1, waiting for transfers between devices: 0.55 us -> 0.36 us  [per_device(): xs.append(lax.ppermute(x_piece, 'row', [(i ^ k, i) for i in range(n_row)]))]
  transfers between devices with their start and end apart: 8 -> 8, of which waited for: 3 -> 4; matrix products, arithmetic and copies ran while one was open for 0% -> 0% of each run, Pallas kernels for 2% -> 2%
where the time goes in v3:
time: 14.9 us; the launch traced here: 14.7 us
  starting transfers between devices  9.11 us (61%)
  waiting for transfers between devices  3.28 us (22%)
  Pallas kernels  2.29 us (15%)
    ppermute x4, starting transfers between devices, swap(): return lax.ppermute(value, ('col', 'layer'), pairs)  7.36 us
    ppermute x4, waiting for transfers between devices, swap(): return lax.ppermute(value, ('col', 'layer'), pairs)  2.92 us
    ppermute x1, starting transfers between devices, per_device(): xs.append(lax.ppermute(x_piece, 'row', [(i ^ k, i) for i in range(n_row)]))  1.58 us
    pallas_call x1, Pallas kernels, per_device(): pl.pallas_call(functools.partial(final_kernel, sizes), out_shape=jax.Shap...  1.1 us
    pallas_call x1, Pallas kernels, per_device(): pl.pallas_call(pack_kernel, out_shape=(pltpu.VMEM((slots * block + TAIL,...  0.86 us
    ppermute x1, waiting for transfers between devices, per_device(): xs.append(lax.ppermute(x_piece, 'row', [(i ^ k, i) for i in range(n_row)]))  0.36 us
    pallas_call x1, Pallas kernels, per_device(): pl.pallas_call(functools.partial(early_kernel, sizes), out_shape=(pltpu.V...  0.33 us
  transfers between devices with their start and end apart: 8, of which 4 were waited for; matrix products, arithmetic and copies ran while one was open for 0% of the time, Pallas kernels for 2%

profile of v3, /device:TPU:0, one launch (start us, length us, event | category | flops | bytes accessed | tf_op | source)
XLA Modules:
  0.0 14.7 jit_solution(8398941843840797969)
XLA Ops:
  0.0 0.0 copy-start
  0.0 0.9 %shard_map.46 = (bf16[272,128]{1,0:T(8,128)(2,1)S(1)}, bf16[16,128]{1,0:T(8,128)(2,1)S(1)}) custom-call(bf16[256,128]{1,0:T(8,128)(2,1)} %bitcast.5, s32[2]{0:T(128)} %bitcast.6, s32[4]{0:T(128)} %bitcast.7), custom_call_target="tpu_custom_call" | custom-call | flops 1000000000 | bytes 1000000 | tf_op jit(solution)/shard_map/pallas_call | solution.py:124
  0.9 5.1 %collective-permute-start.1 = (bf16[272,128]{1,0:T(8,128)(2,1)S(1)}, bf16[272,128]{1,0:T(8,128)(2,1)S(1)}, u32[]{:S(2)}, u32[]{:S(2)}) collective-permute-start(bf16[272,128]{1,0:T(8,128)(2,1)S(1)} %get-tuple-element.11.refs_2_), channel_id=1, source_target_pairs={{0,12},{1,15},{2,14},{3,13},{4,8},{5,11},{6,10},{7,9},{8,4},{9,7},... | collective-permute-start | bytes 208904 | tf_op jit(solution)/shard_map/ppermute | solution.py:112
  6.0 0.0 collective-permute-start.2
  6.0 1.7 %collective-permute-start.3 = (bf16[272,128]{1,0:T(8,128)(2,1)S(1)}, bf16[272,128]{1,0:T(8,128)(2,1)S(1)}, u32[]{:S(2)}, u32[]{:S(2)}) collective-permute-start(bf16[272,128]{1,0:T(8,128)(2,1)S(1)} %get-tuple-element.11.refs_2_), channel_id=1, source_target_pairs={{0,10},{1,7},{2,8},{3,5},{4,14},{5,3},{6,12},{7,1},{8,2},{9,15},{1... | collective-permute-start | bytes 208904 | tf_op jit(solution)/shard_map/ppermute | solution.py:112
  7.7 0.0 copy-done
  7.7 1.6 %collective-permute-start = (bf16[528,128]{1,0:T(8,128)(2,1)S(1)}, bf16[528,128]{1,0:T(8,128)(2,1)S(1)}, u32[]{:S(2)}, u32[]{:S(2)}) collective-permute-start(bf16[528,128]{1,0:T(8,128)(2,1)S(1)} %shard_map.47.refs_0_), channel_id=1, source_target_pairs={{16,0},{0,16},{17,1},{1,17},{18,2},{2,18},{19,3},{3,19},{20,4},{4,... | collective-permute-start | bytes 405512 | tf_op jit(solution)/shard_map/ppermute | solution.py:152
  9.3 0.5 %collective-permute-start.4 = (bf16[272,128]{1,0:T(8,128)(2,1)S(1)}, bf16[272,128]{1,0:T(8,128)(2,1)S(1)}, u32[]{:S(2)}, u32[]{:S(2)}) collective-permute-start(bf16[272,128]{1,0:T(8,128)(2,1)S(1)} %get-tuple-element.11.refs_2_), channel_id=1, source_target_pairs={{0,2},{1,3},{2,0},{3,1},{4,6},{5,7},{6,4},{7,5},{8,10},{9,11},{10,... | collective-permute-start | bytes 208904 | tf_op jit(solution)/shard_map/ppermute | solution.py:112
  9.8 0.0 collective-permute-done.1.refs_3_
  9.8 0.0 collective-permute-start.5
  9.8 1.5 %collective-permute-done.2.refs_4_ = bf16[272,128]{1,0:T(8,128)(2,1)S(1)} collective-permute-done((bf16[272,128]{1,0:T(8,128)(2,1)S(1)}, bf16[272,128]{1,0:T(8,128)(2,1)S(1)}, u32[]{:S(2)}, u32[]{:S(2)}) %collective-permute-start.2) | collective-permute-done | bytes 69664 | tf_op jit(solution)/shard_map/ppermute | solution.py:112
  11.4 0.0 collective-permute-start.6
  11.4 0.9 %collective-permute-done.3.refs_5_ = bf16[272,128]{1,0:T(8,128)(2,1)S(1)} collective-permute-done((bf16[272,128]{1,0:T(8,128)(2,1)S(1)}, bf16[272,128]{1,0:T(8,128)(2,1)S(1)}, u32[]{:S(2)}, u32[]{:S(2)}) %collective-permute-start.3) | collective-permute-done | bytes 69664 | tf_op jit(solution)/shard_map/ppermute | solution.py:112
  12.3 0.2 %collective-permute-start.7 = (bf16[272,128]{1,0:T(8,128)(2,1)S(1)}, bf16[272,128]{1,0:T(8,128)(2,1)S(1)}, u32[]{:S(2)}, u32[]{:S(2)}) collective-permute-start(bf16[272,128]{1,0:T(8,128)(2,1)S(1)} %collective-permute-done.3.refs_5_), channel_id=1, source_target_pairs={{0,1},{1,0},{2,3},{3,2},{4,5},{5,4},{6,7},{7,6},{8,9},{9,8},{10,11... | collective-permute-start | bytes 208904 | tf_op jit(solution)/shard_map/ppermute | solution.py:155
  12.4 0.4 %collective-permute-done.refs_1_ = bf16[528,128]{1,0:T(8,128)(2,1)S(1)} collective-permute-done((bf16[528,128]{1,0:T(8,128)(2,1)S(1)}, bf16[528,128]{1,0:T(8,128)(2,1)S(1)}, u32[]{:S(2)}, u32[]{:S(2)}) %collective-permute-start) | collective-permute-done | bytes 135200 | tf_op jit(solution)/shard_map/ppermute | solution.py:152
  12.8 0.3 %shard_map.48 = (f32[512,256]{1,0:T(8,128)S(1)}, bf16[8,128,128]{2,1,0:T(8,128)(2,1)S(1)}, s32[8]{0:T(128)S(4)}) custom-call(bf16[528,128]{1,0:T(8,128)(2,1)S(1)} %shard_map.47.refs_0_, bf16[528,128]{1,0:T(8,128)(2,1)S(1)} %collective-permute-done.refs_1_, bf16[272,128]{1,0:T(8,128)(2,1)S(1)} %get-tuple-element.11.refs_2_, ...), custom_call_target="tpu_custom_call" | custom-call | tf_op jit(solution)/shard_map/pallas_call | solution.py:160
  13.1 0.5 %collective-permute-done.4.refs_0_ = bf16[272,128]{1,0:T(8,128)(2,1)S(1)} collective-permute-done((bf16[272,128]{1,0:T(8,128)(2,1)S(1)}, bf16[272,128]{1,0:T(8,128)(2,1)S(1)}, u32[]{:S(2)}, u32[]{:S(2)}) %collective-permute-start.4) | collective-permute-done | bytes 69664 | tf_op jit(solution)/shard_map/ppermute | solution.py:112
  13.6 0.0 collective-permute-done.5.refs_1_
  13.6 0.0 collective-permute-done.6.refs_2_
  13.6 0.0 collective-permute-done.7.refs_3_
  13.6 1.1 %shard_map.49 = f32[512,256]{1,0:T(8,128)} custom-call(s32[8]{0:T(128)S(4)} %get-tuple-element.12.x_at, bf16[8,128,128]{2,1,0:T(8,128)(2,1)S(1)} %get-tuple-element.13.x_all, f32[512,256]{1,0:T(8,128)S(1)} %get-tuple-element.14.total, bf16[272,128]{1,0:T(8,128)(2,1)S(1)} %collective-permute-done.4.refs_0_, ...), custom_call_target="tpu_custom_call" | custom-call | tf_op jit(solution)/shard_map/pallas_call | solution.py:171
  (1 shorter events, 0.0 us)
Async XLA Ops:
  0.0 7.7 %copy-start = (bf16[4,1,1,1,128,128]{5,4,3,2,1,0:T(8,128)(2,1)S(1)}, bf16[4,1,1,1,128,128]{5,4,3,2,1,0:T(8,128)(2,1)}, u32[]{:S(2)}) copy-start(bf16[4,1,1,1,128,128]{5,4,3,2,1,0:T(8,128)(2,1)} %param.6) | copy-start | bytes 393220
  0.9 9.0 %collective-permute-start.1 = (bf16[272,128]{1,0:T(8,128)(2,1)S(1)}, bf16[272,128]{1,0:T(8,128)(2,1)S(1)}, u32[]{:S(2)}, u32[]{:S(2)}) collective-permute-start(bf16[272,128]{1,0:T(8,128)(2,1)S(1)} %get-tuple-element.11.refs_2_), channel_id=1, source_target_pairs={{0,12},{1,15},{2,14},{3,13},{4,8},{5,11},{6,10},{7,9},{8,4},{9,7},... | collective-permute-start | bytes 208904 | tf_op jit(solution)/shard_map/ppermute | solution.py:112
  6.0 5.4 %collective-permute-start.2 = (bf16[272,128]{1,0:T(8,128)(2,1)S(1)}, bf16[272,128]{1,0:T(8,128)(2,1)S(1)}, u32[]{:S(2)}, u32[]{:S(2)}) collective-permute-start(bf16[272,128]{1,0:T(8,128)(2,1)S(1)} %get-tuple-element.11.refs_2_), channel_id=1, source_target_pairs={{0,4},{1,9},{2,6},{3,11},{4,0},{5,13},{6,2},{7,15},{8,12},{9,1},{1... | collective-permute-start | bytes 208904 | tf_op jit(solution)/shard_map/ppermute | solution.py:112
  6.0 6.3 %collective-permute-start.3 = (bf16[272,128]{1,0:T(8,128)(2,1)S(1)}, bf16[272,128]{1,0:T(8,128)(2,1)S(1)}, u32[]{:S(2)}, u32[]{:S(2)}) collective-permute-start(bf16[272,128]{1,0:T(8,128)(2,1)S(1)} %get-tuple-element.11.refs_2_), channel_id=1, source_target_pairs={{0,10},{1,7},{2,8},{3,5},{4,14},{5,3},{6,12},{7,1},{8,2},{9,15},{1... | collective-permute-start | bytes 208904 | tf_op jit(solution)/shard_map/ppermute | solution.py:112
  7.7 5.1 %collective-permute-start = (bf16[528,128]{1,0:T(8,128)(2,1)S(1)}, bf16[528,128]{1,0:T(8,128)(2,1)S(1)}, u32[]{:S(2)}, u32[]{:S(2)}) collective-permute-start(bf16[528,128]{1,0:T(8,128)(2,1)S(1)} %shard_map.47.refs_0_), channel_id=1, source_target_pairs={{16,0},{0,16},{17,1},{1,17},{18,2},{2,18},{19,3},{3,19},{20,4},{4,... | collective-permute-start | bytes 405512 | tf_op jit(solution)/shard_map/ppermute | solution.py:152
  9.3 4.3 %collective-permute-start.4 = (bf16[272,128]{1,0:T(8,128)(2,1)S(1)}, bf16[272,128]{1,0:T(8,128)(2,1)S(1)}, u32[]{:S(2)}, u32[]{:S(2)}) collective-permute-start(bf16[272,128]{1,0:T(8,128)(2,1)S(1)} %get-tuple-element.11.refs_2_), channel_id=1, source_target_pairs={{0,2},{1,3},{2,0},{3,1},{4,6},{5,7},{6,4},{7,5},{8,10},{9,11},{10,... | collective-permute-start | bytes 208904 | tf_op jit(solution)/shard_map/ppermute | solution.py:112
  9.8 3.8 %collective-permute-start.5 = (bf16[272,128]{1,0:T(8,128)(2,1)S(1)}, bf16[272,128]{1,0:T(8,128)(2,1)S(1)}, u32[]{:S(2)}, u32[]{:S(2)}) collective-permute-start(bf16[272,128]{1,0:T(8,128)(2,1)S(1)} %collective-permute-done.1.refs_3_), channel_id=1, source_target_pairs={{0,1},{1,0},{2,3},{3,2},{4,5},{5,4},{6,7},{7,6},{8,9},{9,8},{10,11... | collective-permute-start | bytes 208904 | tf_op jit(solution)/shard_map/ppermute | solution.py:155
  11.4 2.3 %collective-permute-start.6 = (bf16[272,128]{1,0:T(8,128)(2,1)S(1)}, bf16[272,128]{1,0:T(8,128)(2,1)S(1)}, u32[]{:S(2)}, u32[]{:S(2)}) collective-permute-start(bf16[272,128]{1,0:T(8,128)(2,1)S(1)} %collective-permute-done.2.refs_4_), channel_id=1, source_target_pairs={{0,1},{1,0},{2,3},{3,2},{4,5},{5,4},{6,7},{7,6},{8,9},{9,8},{10,11... | collective-permute-start | bytes 208904 | tf_op jit(solution)/shard_map/ppermute | solution.py:155
  12.3 1.3 %collective-permute-start.7 = (bf16[272,128]{1,0:T(8,128)(2,1)S(1)}, bf16[272,128]{1,0:T(8,128)(2,1)S(1)}, u32[]{:S(2)}, u32[]{:S(2)}) collective-permute-start(bf16[272,128]{1,0:T(8,128)(2,1)S(1)} %collective-permute-done.3.refs_5_), channel_id=1, source_target_pairs={{0,1},{1,0},{2,3},{3,2},{4,5},{5,4},{6,7},{7,6},{8,9},{9,8},{10,11... | collective-permute-start | bytes 208904 | tf_op jit(solution)/shard_map/ppermute | solution.py:155

commit v4 on v2

--- a/solution.py
+++ b/solution.py
@@ -57,14 +57,16 @@
     s_at = [slots_of(ref, slots) for ref, _ in pieces]
     for first in range(0, len(pieces), 2):
         pair = pieces[first : first + 2]
-        x0, x1 = [x_all[piece] for _, piece in pair]
-        right = jnp.concatenate(
-            [
-                jnp.concatenate([x0, zero], axis=1),
-                jnp.concatenate([zero, x1], axis=1),
-            ],
-            axis=0,
-        )
+        values = [x_all[piece] for _, piece in pair]
+        right = values[0]
+        if len(pair) == 2:
+            right = jnp.concatenate(
+                [
+                    jnp.concatenate([values[0], zero], axis=1),
+                    jnp.concatenate([zero, values[1]], axis=1),
+                ],
+                axis=0,
+            )
         left = jnp.concatenate([ref[: slots * block] for ref, _ in pair], axis=1)
         tiles = jnp.dot(left, right, preferred_element_type=jnp.float32)
         for e, (_, piece) in enumerate(pair):
@@ -78,18 +80,28 @@
                 total[rows, columns] += jnp.where(live, tile, 0.0)
 
 
-def early_kernel(sizes, *refs):
+def lay_out(sizes, k, ref, x_all):
+    n_row, _, _, _, q = sizes
+    block = x_all.shape[-1]
+    for m in range(q):
+        x_all[m * n_row + (lax.axis_index("row") ^ k)] = ref[m * block : (m + 1) * block]
+
+
+def prepare_kernel(sizes, x_ref, total, x_all):
+    total[...] = jnp.zeros_like(total)
+    lay_out(sizes, 0, x_ref, x_all)
+
+
+def early_kernel(sizes, _, __, *refs):
     n_row, n_col, inner, slots, q = sizes
-    x_refs, s_refs = refs[:n_row], refs[n_row : n_row + n_col // 2]
-    total, x_all, x_at = refs[n_row + n_col // 2 :]
+    x_refs, s_refs = refs[:n_row], refs[n_row:-3]
+    total, x_all, x_at = refs[-3:]
     row, col, layer = lax.axis_index("row"), lax.axis_index("col"), lax.axis_index("layer")
-    block = x_all.shape[-1]
     for k, ref in enumerate(x_refs):
+        if k:
+            lay_out(sizes, k, ref, x_all)
         for m, slot in enumerate(slots_of(ref, q)):
-            piece = m * n_row + (row ^ k)
-            x_all[piece] = ref[m * block : (m + 1) * block]
-            x_at[piece] = slot
-    total[...] = jnp.zeros_like(total)
+            x_at[m * n_row + (row ^ k)] = slot
     masks = [0] + [one + layer * (two - one) for one, two in swap_order(n_col)]
     pieces = [(ref, col ^ mask) for ref, mask in zip(s_refs, masks)]
     add_products(total, pieces, x_all, x_at, slots, inner)
@@ -157,17 +169,30 @@
     params = pltpu.CompilerParams(vmem_limit_bytes=24 << 20)
     sizes = (n_row, n_col, n_row * BR // n_col, slots, q)
     shape = (BR // n_layer * block, BC * block)
+    prepared = (
+        pltpu.VMEM(shape, jnp.float32),
+        pltpu.VMEM((q * n_row, block, block), jnp.bfloat16),
+    )
+    started = pl.pallas_call(
+        functools.partial(prepare_kernel, sizes),
+        out_shape=prepared,
+        in_specs=[vmem],
+        out_specs=(vmem, vmem),
+        compiler_params=params,
+    )(x_piece)
     total, x_all, x_at = pl.pallas_call(
         functools.partial(early_kernel, sizes),
-        out_shape=(
-            pltpu.VMEM(shape, jnp.float32),
-            pltpu.VMEM((q * n_row, block, block), jnp.bfloat16),
-            pltpu.SMEM((q * n_row,), jnp.int32),
-        ),
-        in_specs=[vmem] * (n_row + 1 + len(fetched)),
+        out_shape=(*prepared, pltpu.SMEM((q * n_row,), jnp.int32)),
+        in_specs=[vmem] * (n_row + 3 + len(fetched)),
         out_specs=(vmem, vmem, smem),
-        compiler_params=params,
-    )(*xs, s_piece, *fetched)
+        input_output_aliases={0: 0, 1: 1},
+        compiler_params=params,
+    )(
+        *[pltpu.with_memory_space_constraint(array, pltpu.VMEM) for array in started],
+        *xs,
+        s_piece,
+        *fetched,
+    )
     return pl.pallas_call(
         functools.partial(final_kernel, sizes),
         out_shape=jax.ShapeDtypeStruct(shape, jnp.float32),

time: 14.8 us -> 14.8 us (level)
    pallas_call x1 -> x2, Pallas kernels: 0.32 us -> 0.35 us  [the longest x1 0.31 us: per_device(): pl.pallas_call(functools.partial(early_kernel, sizes), out_shape=(*prepar...]
where the time goes in v4:
time: 14.8 us; the launch traced here: 14.6 us
  starting transfers between devices  9.35 us (63%)
  waiting for transfers between devices  2.9 us (20%)
  Pallas kernels  2.31 us (16%)
    ppermute x4, starting transfers between devices, swap(): return lax.ppermute(value, ('col', 'layer'), pairs)  7.25 us
    ppermute x4, waiting for transfers between devices, swap(): return lax.ppermute(value, ('col', 'layer'), pairs)  2.38 us
    ppermute x1, starting transfers between devices, per_device(): xs.append(lax.ppermute(x_piece, 'row', [(i ^ k, i) for i in range(n_row)]))  1.73 us
    pallas_call x1, Pallas kernels, per_device(): pl.pallas_call(functools.partial(final_kernel, sizes), out_shape=jax.Shap...  1.09 us
    pallas_call x1, Pallas kernels, per_device(): pl.pallas_call(pack_kernel, out_shape=(pltpu.VMEM((slots * block + TAIL,...  0.86 us
    ppermute x1, waiting for transfers between devices, per_device(): xs.append(lax.ppermute(x_piece, 'row', [(i ^ k, i) for i in range(n_row)]))  0.5 us
    ppermute x3, starting transfers between devices, per_device(): handed = [lax.ppermute(piece, 'layer', over) for piece in fetched]  0.37 us
    pallas_call x1, Pallas kernels, per_device(): pl.pallas_call(functools.partial(early_kernel, sizes), out_shape=(*prepar...  0.31 us
  transfers between devices with their start and end apart: 8, of which 3 were waited for; matrix products, arithmetic and copies ran while one was open for 0% of the time, Pallas kernels for 2%

profile of v4, /device:TPU:0, one launch (start us, length us, event | category | flops | bytes accessed | tf_op | source)
XLA Modules:
  0.0 14.6 jit_solution(4810056692181279434)
XLA Ops:
  0.0 0.0 copy-start
  0.0 0.9 %shard_map.46 = (bf16[272,128]{1,0:T(8,128)(2,1)S(1)}, bf16[16,128]{1,0:T(8,128)(2,1)S(1)}) custom-call(bf16[256,128]{1,0:T(8,128)(2,1)} %bitcast.5, s32[2]{0:T(128)} %bitcast.6, s32[4]{0:T(128)} %bitcast.7), custom_call_target="tpu_custom_call" | custom-call | flops 1000000000 | bytes 1000000 | tf_op jit(solution)/shard_map/pallas_call | solution.py:136
  0.9 5.1 %collective-permute-start.1 = (bf16[272,128]{1,0:T(8,128)(2,1)S(1)}, bf16[272,128]{1,0:T(8,128)(2,1)S(1)}, u32[]{:S(2)}, u32[]{:S(2)}) collective-permute-start(bf16[272,128]{1,0:T(8,128)(2,1)S(1)} %get-tuple-element.15.refs_2_), channel_id=1, source_target_pairs={{0,12},{1,15},{2,14},{3,13},{4,8},{5,11},{6,10},{7,9},{8,4},{9,7},... | collective-permute-start | bytes 208904 | tf_op jit(solution)/shard_map/ppermute | solution.py:124
  6.0 0.0 collective-permute-start.2
  6.0 0.6 %collective-permute-start.3 = (bf16[272,128]{1,0:T(8,128)(2,1)S(1)}, bf16[272,128]{1,0:T(8,128)(2,1)S(1)}, u32[]{:S(2)}, u32[]{:S(2)}) collective-permute-start(bf16[272,128]{1,0:T(8,128)(2,1)S(1)} %get-tuple-element.15.refs_2_), channel_id=1, source_target_pairs={{0,8},{1,7},{2,10},{3,5},{4,12},{5,3},{6,14},{7,1},{8,0},{9,15},{1... | collective-permute-start | bytes 208904 | tf_op jit(solution)/shard_map/ppermute | solution.py:124
  6.6 0.0 copy-done
  6.6 1.7 %collective-permute-start = (bf16[528,128]{1,0:T(8,128)(2,1)S(1)}, bf16[528,128]{1,0:T(8,128)(2,1)S(1)}, u32[]{:S(2)}, u32[]{:S(2)}) collective-permute-start(bf16[528,128]{1,0:T(8,128)(2,1)S(1)} %shard_map.47.x_ref.refs_0_), channel_id=1, source_target_pairs={{16,0},{0,16},{17,1},{1,17},{18,2},{2,18},{19,3},{3,19},{20,4},{4,... | collective-permute-start | bytes 405512 | tf_op jit(solution)/shard_map/ppermute | solution.py:164
  8.4 1.5 %collective-permute-start.4 = (bf16[272,128]{1,0:T(8,128)(2,1)S(1)}, bf16[272,128]{1,0:T(8,128)(2,1)S(1)}, u32[]{:S(2)}, u32[]{:S(2)}) collective-permute-start(bf16[272,128]{1,0:T(8,128)(2,1)S(1)} %get-tuple-element.15.refs_2_), channel_id=1, source_target_pairs={{0,2},{1,3},{2,0},{3,1},{4,6},{5,7},{6,4},{7,5},{8,10},{9,11},{10,... | collective-permute-start | bytes 208904 | tf_op jit(solution)/shard_map/ppermute | solution.py:124
  9.9 0.0 collective-permute-done.1.refs_3_
  9.9 0.0 collective-permute-start.5
  9.9 2.2 %collective-permute-done.2.refs_4_ = bf16[272,128]{1,0:T(8,128)(2,1)S(1)} collective-permute-done((bf16[272,128]{1,0:T(8,128)(2,1)S(1)}, bf16[272,128]{1,0:T(8,128)(2,1)S(1)}, u32[]{:S(2)}, u32[]{:S(2)}) %collective-permute-start.2) | collective-permute-done | bytes 69664 | tf_op jit(solution)/shard_map/ppermute | solution.py:124
  12.1 0.0 collective-permute-start.6
  12.1 0.1 collective-permute-done.3.refs_5_
  12.2 0.4 %collective-permute-start.7 = (bf16[272,128]{1,0:T(8,128)(2,1)S(1)}, bf16[272,128]{1,0:T(8,128)(2,1)S(1)}, u32[]{:S(2)}, u32[]{:S(2)}) collective-permute-start(bf16[272,128]{1,0:T(8,128)(2,1)S(1)} %collective-permute-done.3.refs_5_), channel_id=1, source_target_pairs={{0,1},{1,0},{2,3},{3,2},{4,5},{5,4},{6,7},{7,6},{8,9},{9,8},{10,11... | collective-permute-start | bytes 208904 | tf_op jit(solution)/shard_map/ppermute | solution.py:167
  12.7 0.5 %collective-permute-done.refs_1_ = bf16[528,128]{1,0:T(8,128)(2,1)S(1)} collective-permute-done((bf16[528,128]{1,0:T(8,128)(2,1)S(1)}, bf16[528,128]{1,0:T(8,128)(2,1)S(1)}, u32[]{:S(2)}, u32[]{:S(2)}) %collective-permute-start) | collective-permute-done | bytes 135200 | tf_op jit(solution)/shard_map/ppermute | solution.py:164
  13.2 0.3 %shard_map.49 = (f32[512,256]{1,0:T(8,128)S(1)}, bf16[8,128,128]{2,1,0:T(8,128)(2,1)S(1)}, s32[8]{0:T(128)S(4)}) custom-call(f32[512,256]{1,0:T(8,128)S(1)} %get-tuple-element.13._, bf16[8,128,128]{2,1,0:T(8,128)(2,1)S(1)} %get-tuple-element.14.__, bf16[528,128]{1,0:T(8,128)(2,1)S(1)} %shard_map.47.x_ref.refs_0_, ...), custom_call_target="tpu_custom_call", output_to_operand_aliasing={{0}: (0, {}), {1}: (1, {})} | custom-call | tf_op jit(solution)/shard_map/pallas_call | solution.py:183
  13.5 0.0 collective-permute-done.4.refs_0_
  13.5 0.0 collective-permute-done.5.refs_1_
  13.5 0.0 collective-permute-done.6.refs_2_
  13.5 0.0 collective-permute-done.7.refs_3_
  13.5 1.1 %shard_map.50 = f32[512,256]{1,0:T(8,128)} custom-call(s32[8]{0:T(128)S(4)} %get-tuple-element.16.x_at, bf16[8,128,128]{2,1,0:T(8,128)(2,1)S(1)} %get-tuple-element.17.x_all, f32[512,256]{1,0:T(8,128)S(1)} %get-tuple-element.18.total, bf16[272,128]{1,0:T(8,128)(2,1)S(1)} %collective-permute-done.4.refs_0_, ...), custom_call_target="tpu_custom_call" | custom-call | tf_op jit(solution)/shard_map/pallas_call | solution.py:196
  (2 shorter events, 0.1 us)
Async XLA Ops:
  0.0 6.6 %copy-start = (bf16[4,1,1,1,128,128]{5,4,3,2,1,0:T(8,128)(2,1)S(1)}, bf16[4,1,1,1,128,128]{5,4,3,2,1,0:T(8,128)(2,1)}, u32[]{:S(2)}) copy-start(bf16[4,1,1,1,128,128]{5,4,3,2,1,0:T(8,128)(2,1)} %param.6) | copy-start | bytes 393220
  0.9 9.0 %collective-permute-start.1 = (bf16[272,128]{1,0:T(8,128)(2,1)S(1)}, bf16[272,128]{1,0:T(8,128)(2,1)S(1)}, u32[]{:S(2)}, u32[]{:S(2)}) collective-permute-start(bf16[272,128]{1,0:T(8,128)(2,1)S(1)} %get-tuple-element.15.refs_2_), channel_id=1, source_target_pairs={{0,12},{1,15},{2,14},{3,13},{4,8},{5,11},{6,10},{7,9},{8,4},{9,7},... | collective-permute-start | bytes 208904 | tf_op jit(solution)/shard_map/ppermute | solution.py:124
  6.0 6.1 %collective-permute-start.2 = (bf16[272,128]{1,0:T(8,128)(2,1)S(1)}, bf16[272,128]{1,0:T(8,128)(2,1)S(1)}, u32[]{:S(2)}, u32[]{:S(2)}) collective-permute-start(bf16[272,128]{1,0:T(8,128)(2,1)S(1)} %get-tuple-element.15.refs_2_), channel_id=1, source_target_pairs={{0,4},{1,11},{2,6},{3,9},{4,0},{5,15},{6,2},{7,13},{8,12},{9,3},{1... | collective-permute-start | bytes 208904 | tf_op jit(solution)/shard_map/ppermute | solution.py:124
  6.0 6.3 %collective-permute-start.3 = (bf16[272,128]{1,0:T(8,128)(2,1)S(1)}, bf16[272,128]{1,0:T(8,128)(2,1)S(1)}, u32[]{:S(2)}, u32[]{:S(2)}) collective-permute-start(bf16[272,128]{1,0:T(8,128)(2,1)S(1)} %get-tuple-element.15.refs_2_), channel_id=1, source_target_pairs={{0,8},{1,7},{2,10},{3,5},{4,12},{5,3},{6,14},{7,1},{8,0},{9,15},{1... | collective-permute-start | bytes 208904 | tf_op jit(solution)/shard_map/ppermute | solution.py:124
  6.6 6.5 %collective-permute-start = (bf16[528,128]{1,0:T(8,128)(2,1)S(1)}, bf16[528,128]{1,0:T(8,128)(2,1)S(1)}, u32[]{:S(2)}, u32[]{:S(2)}) collective-permute-start(bf16[528,128]{1,0:T(8,128)(2,1)S(1)} %shard_map.47.x_ref.refs_0_), channel_id=1, source_target_pairs={{16,0},{0,16},{17,1},{1,17},{18,2},{2,18},{19,3},{3,19},{20,4},{4,... | collective-permute-start | bytes 405512 | tf_op jit(solution)/shard_map/ppermute | solution.py:164
  8.4 5.1 %collective-permute-start.4 = (bf16[272,128]{1,0:T(8,128)(2,1)S(1)}, bf16[272,128]{1,0:T(8,128)(2,1)S(1)}, u32[]{:S(2)}, u32[]{:S(2)}) collective-permute-start(bf16[272,128]{1,0:T(8,128)(2,1)S(1)} %get-tuple-element.15.refs_2_), channel_id=1, source_target_pairs={{0,2},{1,3},{2,0},{3,1},{4,6},{5,7},{6,4},{7,5},{8,10},{9,11},{10,... | collective-permute-start | bytes 208904 | tf_op jit(solution)/shard_map/ppermute | solution.py:124
  9.9 3.6 %collective-permute-start.5 = (bf16[272,128]{1,0:T(8,128)(2,1)S(1)}, bf16[272,128]{1,0:T(8,128)(2,1)S(1)}, u32[]{:S(2)}, u32[]{:S(2)}) collective-permute-start(bf16[272,128]{1,0:T(8,128)(2,1)S(1)} %collective-permute-done.1.refs_3_), channel_id=1, source_target_pairs={{0,1},{1,0},{2,3},{3,2},{4,5},{5,4},{6,7},{7,6},{8,9},{9,8},{10,11... | collective-permute-start | bytes 208904 | tf_op jit(solution)/shard_map/ppermute | solution.py:167
  12.1 1.4 %collective-permute-start.6 = (bf16[272,128]{1,0:T(8,128)(2,1)S(1)}, bf16[272,128]{1,0:T(8,128)(2,1)S(1)}, u32[]{:S(2)}, u32[]{:S(2)}) collective-permute-start(bf16[272,128]{1,0:T(8,128)(2,1)S(1)} %collective-permute-done.2.refs_4_), channel_id=1, source_target_pairs={{0,1},{1,0},{2,3},{3,2},{4,5},{5,4},{6,7},{7,6},{8,9},{9,8},{10,11... | collective-permute-start | bytes 208904 | tf_op jit(solution)/shard_map/ppermute | solution.py:167
  12.2 1.3 %collective-permute-start.7 = (bf16[272,128]{1,0:T(8,128)(2,1)S(1)}, bf16[272,128]{1,0:T(8,128)(2,1)S(1)}, u32[]{:S(2)}, u32[]{:S(2)}) collective-permute-start(bf16[272,128]{1,0:T(8,128)(2,1)S(1)} %collective-permute-done.3.refs_5_), channel_id=1, source_target_pairs={{0,1},{1,0},{2,3},{3,2},{4,5},{5,4},{6,7},{7,6},{8,9},{9,8},{10,11... | collective-permute-start | bytes 208904 | tf_op jit(solution)/shard_map/ppermute | solution.py:167
